TPU v7x, 32 devices: a whole 2x2x4 slice. The times are simulated.
32 devices in a mesh: section: 2 (over x), wide: 16 (over z, y, core).
Axes of the slice: x: 2, y: 2, z: 4, core: 2. Of those that a mesh axis runs over, the one named last changes fastest.
Arguments:
- tokens: bfloat16 [8192, 768], P('wide'), may hold values from -6 to 6
- cotangent: bfloat16 [8192, 768], P('wide'), may hold values from -6 to 6
- lengths: int32 [32], P('wide'), may hold values from 16 to 256, as said below
- buckets: int32 [3, 8192], P(None, 'wide'), may hold values from 0 to 31
- in_proj: bfloat16 [2, 768, 2304], P('section'), may hold values from -0.21875 to 0.21875
- out_proj: bfloat16 [2, 768, 768], P('section'), may hold values from -0.625 to 0.625
- up_proj: bfloat16 [2, 768, 3072], P('section'), may hold values from -0.21875 to 0.21875
- down_proj: bfloat16 [2, 3072, 768], P('section'), may hold values from -0.109375 to 0.109375
- layout_tables: bfloat16 [2, 3, 12, 1024], P('section'), may hold values from -3 to 3
- norm_gains: float32 [2, 2, 768], P('section'), may hold values from 0.5 to 1.5
- offsets: float32 [2, 6, 768], P('section'), may hold values from -2 to 2
- hidden_bias: float32 [2, 3072], P('section'), may hold values from -2 to 2
Outputs:
- section_outputs: bfloat16 [2, 8192, 768], P('section', 'wide')
- section_input_grads: float32 [2, 8192, 768], P('section', 'wide')
- grad_in_proj: float32 [2, 768, 2304], P('section', 'wide')
- grad_out_proj: float32 [2, 768, 768], P('section', 'wide')
- grad_up_proj: float32 [2, 768, 3072], P('section', 'wide')
- grad_down_proj: float32 [2, 3072, 768], P('section', 'wide')
- grad_layout_tables: float32 [2, 3, 12, 1024], P('section', None, None, 'wide')
- grad_norm_gains: float32 [2, 2, 768], P('section', None, 'wide')
- grad_offsets: float32 [2, 6, 768], P('section', None, 'wide')
- grad_hidden_bias: float32 [2, 3072], P('section', 'wide')
Inputs may be any that keep to these rules, and one draw needn't show every extreme that they name: `lengths`: page positions below a page's length hold real tokens; some page has exactly 256.
All inputs are finite; a program needn't handle non-finite values.
Results may differ from a plain program's by a relative error of at most 0.023.
Values may be sent and summed in bfloat16 or wider, within the bound.
A program may use at most 448 MiB of HBM per device.

v0:
```python
import jax
import jax.numpy as jnp
from jax import lax
from jax.sharding import PartitionSpec as P

BUCKETS = 32


epsilon = 1e-05
masked_score = -1000000000.0


def from_behind(value, axis, steps):
    count = lax.axis_size(axis)
    initial, last = (max(0, -steps), min(count, count - steps))
    return lax.ppermute(value, axis, [(source, source + steps) for source in range(initial, last)])


def normalize(values, gain, offset):
    centered = values - jnp.mean(values, axis=-1, keepdims=True)
    spread = jnp.mean(centered * centered, axis=-1, keepdims=True)
    return centered * lax.rsqrt(spread + epsilon) * gain + offset


def gelu_exact(values):
    return jax.nn.gelu(values, approximate=False)


def contract_rows(left, right):
    return lax.dot_general(
        left, right, (((0,), (0,)), ((), ())), preferred_element_type=jnp.float32
    )


def contract_cols(left, right):
    return lax.dot_general(
        left, right, (((1,), (1,)), ((), ())), preferred_element_type=jnp.float32
    )


def layout_bias(tables, onehot):
    axis_count, head_count, cell_count = tables.shape
    bucket_count = onehot.shape[2]
    grid = tables.reshape(axis_count, head_count, bucket_count, bucket_count)
    picked = jnp.einsum("aqi,ahij->ahqj", onehot, grid, preferred_element_type=jnp.float32).astype(
        jnp.bfloat16
    )
    return jnp.einsum("ahqj,akj->hqk", picked, onehot, preferred_element_type=jnp.float32)


def split_heads(projected, head_count):
    row_count, triple = projected.shape
    width = triple // 3
    head_size = width // head_count
    query = projected[:, :width].reshape(row_count, head_count, head_size)
    keyed = projected[:, width : 2 * width].reshape(row_count, head_count, head_size)
    valued = projected[:, 2 * width :].reshape(row_count, head_count, head_size)
    return (query, keyed, valued)


def score_block(query, keyed, layout, key_live):
    scaling = query.shape[2] ** (-0.5)
    scores = (
        jnp.einsum("qhe,khe->hqk", query, keyed, preferred_element_type=jnp.float32) * scaling
        + layout
    )
    return jnp.where(key_live[None, None, :], scores, masked_score)


def page_forward(layer_in, key_live, onehot, params):
    in_proj, out_proj, up_proj, down_proj, tables, gains, offsets, hidden_bias = params
    row_count, width = layer_in.shape
    head_count = tables.shape[1]
    blank = jnp.zeros((width,), jnp.float32)
    projected = jnp.dot(layer_in, in_proj, preferred_element_type=jnp.float32) + jnp.concatenate(
        [offsets[0], blank, offsets[1]]
    )
    projected = projected.astype(jnp.bfloat16)
    query, keyed, valued = split_heads(projected, head_count)
    layout = layout_bias(tables, onehot)
    scores = score_block(query, keyed, layout, key_live)
    peak = jnp.max(scores, axis=-1, keepdims=True)
    raised = jnp.exp(scores - peak)
    denom_sum = jnp.sum(raised, axis=-1, keepdims=True)
    attention = raised / denom_sum
    log_norm = (peak + jnp.log(denom_sum))[:, :, 0]
    context = jnp.einsum(
        "hqk,khe->qhe", attention.astype(jnp.bfloat16), valued, preferred_element_type=jnp.float32
    )
    context = context.reshape(row_count, width).astype(jnp.bfloat16)
    attended = jnp.dot(context, out_proj, preferred_element_type=jnp.float32) + offsets[2]
    first_sum = layer_in.astype(jnp.float32) + attended
    normed = normalize(first_sum, gains[0], offsets[3])
    normed_low = normed.astype(jnp.bfloat16)
    before = jnp.dot(normed_low, up_proj, preferred_element_type=jnp.float32) + hidden_bias
    hidden = gelu_exact(before).astype(jnp.bfloat16)
    second_sum = normed + (
        jnp.dot(hidden, down_proj, preferred_element_type=jnp.float32) + offsets[4]
    )
    result = normalize(second_sum, gains[1], offsets[5]).astype(jnp.bfloat16)
    return (result, (projected, log_norm, context, first_sum, normed_low, before, second_sum))


def empty_forward(row_count, width, ff_width, head_count):
    result = jnp.zeros((row_count, width), jnp.bfloat16)
    stored = (
        jnp.zeros((row_count, 3 * width), jnp.bfloat16),
        jnp.zeros((head_count, row_count), jnp.float32),
        jnp.zeros((row_count, width), jnp.bfloat16),
        jnp.zeros((row_count, width), jnp.float32),
        jnp.zeros((row_count, width), jnp.bfloat16),
        jnp.zeros((row_count, ff_width), jnp.float32),
        jnp.zeros((row_count, width), jnp.float32),
    )
    return (result, stored)


def ffn_backward(stored, params, upstream):
    in_proj, out_proj, up_proj, down_proj, tables, gains, offsets, hidden_bias = params
    projected, log_norm, context, first_sum, normed_low, before, second_sum = stored
    _, second_back = jax.vjp(normalize, second_sum, gains[1], offsets[5])
    d_second, d_gain_two, d_offset_five = second_back(upstream)
    d_branch = d_second.astype(jnp.bfloat16)
    activated, gelu_back = jax.vjp(gelu_exact, before)
    hidden = activated.astype(jnp.bfloat16)
    grad_down = contract_rows(hidden, d_branch)
    d_offset_four = jnp.sum(d_branch.astype(jnp.float32), axis=0)
    d_hidden = contract_cols(d_branch, down_proj)
    d_before = gelu_back(d_hidden)[0].astype(jnp.bfloat16)
    grad_up = contract_rows(normed_low, d_before)
    grad_hidden = jnp.sum(d_before.astype(jnp.float32), axis=0)
    d_normed = d_second + contract_cols(d_before, up_proj)
    _, first_back = jax.vjp(normalize, first_sum, gains[0], offsets[3])
    d_first, d_gain_one, d_offset_three = first_back(d_normed)
    grad_gains = jnp.stack([d_gain_one, d_gain_two])
    late_offsets = jnp.stack([d_offset_three, d_offset_four, d_offset_five])
    return (d_first, (grad_up, grad_down, grad_hidden, grad_gains, late_offsets))


def attn_backward(layer_in, key_live, onehot, stored, params, d_first):
    in_proj, out_proj, up_proj, down_proj, tables, gains, offsets, hidden_bias = params
    projected, log_norm, context, first_sum, normed_low, before, second_sum = stored
    row_count, width = layer_in.shape
    head_count = tables.shape[1]
    head_size = width // head_count
    scaling = head_size ** (-0.5)
    d_attended = d_first.astype(jnp.bfloat16)
    grad_out = contract_rows(context, d_attended)
    d_offset_two = jnp.sum(d_attended.astype(jnp.float32), axis=0)
    d_context = (
        contract_cols(d_attended, out_proj)
        .astype(jnp.bfloat16)
        .reshape(row_count, head_count, head_size)
    )
    query, keyed, valued = split_heads(projected, head_count)
    layout = layout_bias(tables, onehot)
    scores = score_block(query, keyed, layout, key_live)
    attention = jnp.exp(scores - log_norm[:, :, None])
    d_attention = jnp.einsum("qhe,khe->hqk", d_context, valued, preferred_element_type=jnp.float32)
    d_scores = attention * (d_attention - jnp.sum(attention * d_attention, axis=-1, keepdims=True))
    d_scores_low = d_scores.astype(jnp.bfloat16)
    d_query = (
        jnp.einsum("hqk,khe->qhe", d_scores_low, keyed, preferred_element_type=jnp.float32)
        * scaling
    )
    d_key = (
        jnp.einsum("hqk,qhe->khe", d_scores_low, query, preferred_element_type=jnp.float32)
        * scaling
    )
    d_value = jnp.einsum(
        "hqk,qhe->khe",
        attention.astype(jnp.bfloat16),
        d_context,
        preferred_element_type=jnp.float32,
    )
    d_projected = jnp.concatenate(
        [
            d_query.reshape(row_count, width),
            d_key.reshape(row_count, width),
            d_value.reshape(row_count, width),
        ],
        axis=1,
    ).astype(jnp.bfloat16)
    grad_in = contract_rows(layer_in, d_projected)
    column_sums = jnp.sum(d_projected.astype(jnp.float32), axis=0)
    early_offsets = jnp.stack([column_sums[:width], column_sums[2 * width :], d_offset_two])
    spread_rows = jnp.einsum(
        "hqk,akj->ahqj", d_scores_low, onehot, preferred_element_type=jnp.float32
    )
    grad_tables = jnp.einsum(
        "aqi,ahqj->ahij", onehot.astype(jnp.float32), spread_rows, precision=lax.Precision.HIGHEST
    ).reshape(3, head_count, -1)
    d_in = d_first + contract_cols(d_projected, in_proj)
    return (d_in, (grad_in, grad_out, grad_tables, early_offsets))


def local(
    tokens,
    cotangent,
    lengths,
    buckets,
    in_proj,
    out_proj,
    up_proj,
    down_proj,
    layout_tables,
    norm_gains,
    offsets,
    hidden_bias,
):
    params = (
        in_proj[0],
        out_proj[0],
        up_proj[0],
        down_proj[0],
        layout_tables[0],
        norm_gains[0],
        offsets[0],
        hidden_bias[0],
    )
    page_count = lengths.shape[0]
    row_count = tokens.shape[0] // page_count
    width = tokens.shape[1]
    head_count = layout_tables.shape[2]
    ff_width = up_proj.shape[2]
    cell_count = layout_tables.shape[3]
    section_index = lax.axis_index("section")
    is_first = section_index == 0
    positions = jnp.arange(row_count, dtype=jnp.int32)
    levels = jnp.arange(BUCKETS, dtype=jnp.int32)

    def page_inputs(moment):
        page_at = jnp.clip(moment - section_index, 0, page_count - 1)
        length = lax.dynamic_slice_in_dim(lengths, page_at, 1)[0]
        bucket_ids = lax.dynamic_slice_in_dim(buckets, page_at * row_count, row_count, 1)
        onehot = (bucket_ids[:, :, None] == levels[None, None, :]).astype(jnp.bfloat16)
        usable = jnp.logical_and(moment - section_index >= 0, moment - section_index < page_count)
        return (positions < length, onehot, usable)

    arriving = jnp.zeros((row_count, width), jnp.bfloat16)
    layer_inputs = []
    stored_all = []
    outputs_at = []
    for moment in range(page_count + 1):
        key_live, onehot, usable = page_inputs(moment)
        if moment < page_count:
            own_page = tokens[moment * row_count : (moment + 1) * row_count]
        else:
            own_page = jnp.zeros((row_count, width), jnp.bfloat16)
        layer_in = jnp.where(is_first, own_page, arriving)
        result, stored = lax.cond(
            usable,
            lambda: page_forward(layer_in, key_live, onehot, params),
            lambda: empty_forward(row_count, width, ff_width, head_count),
        )
        arriving = from_behind(result, "section", 1)
        layer_inputs.append(layer_in)
        stored_all.append(stored)
        outputs_at.append(result)
    totals_ffn = (
        jnp.zeros((width, ff_width), jnp.float32),
        jnp.zeros((ff_width, width), jnp.float32),
        jnp.zeros((ff_width,), jnp.float32),
        jnp.zeros((2, width), jnp.float32),
        jnp.zeros((3, width), jnp.float32),
    )
    totals_attn = (
        jnp.zeros((width, 3 * width), jnp.float32),
        jnp.zeros((width, width), jnp.float32),
        jnp.zeros((3, head_count, cell_count), jnp.float32),
        jnp.zeros((3, width), jnp.float32),
    )
    arriving_grad = jnp.zeros((row_count, width), jnp.bfloat16)
    grads_at = [None] * (page_count + 1)
    for moment in range(page_count, -1, -1):
        key_live, onehot, usable = page_inputs(moment)
        if moment >= 1:
            supplied = cotangent[(moment - 1) * row_count : moment * row_count]
        else:
            supplied = jnp.zeros((row_count, width), jnp.bfloat16)
        upstream = jnp.where(is_first, arriving_grad, supplied).astype(jnp.float32)
        blank_ffn = (
            jnp.zeros((row_count, width), jnp.float32),
            jax.tree.map(jnp.zeros_like, totals_ffn),
        )
        d_first, part_ffn = lax.cond(
            usable, lambda: ffn_backward(stored_all[moment], params, upstream), lambda: blank_ffn
        )
        totals_ffn = jax.tree.map(jnp.add, totals_ffn, part_ffn)
        blank_attn = (
            jnp.zeros((row_count, width), jnp.float32),
            jax.tree.map(jnp.zeros_like, totals_attn),
        )
        d_in, part_attn = lax.cond(
            usable,
            lambda: attn_backward(
                layer_inputs[moment], key_live, onehot, stored_all[moment], params, d_first
            ),
            lambda: blank_attn,
        )
        totals_attn = jax.tree.map(jnp.add, totals_attn, part_attn)
        d_low = d_in.astype(jnp.bfloat16)
        grads_at[moment] = jnp.where(is_first, d_in, d_low.astype(jnp.float32))
        arriving_grad = from_behind(d_low, "section", -1)
    summed = (
        lax.psum_scatter(totals_attn[0][None], "wide", scatter_dimension=1, tiled=True),
        lax.psum_scatter(totals_attn[1][None], "wide", scatter_dimension=1, tiled=True),
        lax.psum_scatter(totals_ffn[0][None], "wide", scatter_dimension=1, tiled=True),
        lax.psum_scatter(totals_ffn[1][None], "wide", scatter_dimension=1, tiled=True),
        lax.psum_scatter(totals_ffn[2][None], "wide", scatter_dimension=1, tiled=True),
        lax.psum_scatter(totals_attn[2][None], "wide", scatter_dimension=3, tiled=True),
        lax.psum_scatter(totals_ffn[3][None], "wide", scatter_dimension=2, tiled=True),
        lax.psum_scatter(totals_attn[3][None], "wide", scatter_dimension=2, tiled=True),
        lax.psum_scatter(totals_ffn[4][None], "wide", scatter_dimension=2, tiled=True),
    )
    (
        grad_in,
        grad_out,
        grad_up,
        grad_down,
        grad_hidden,
        grad_tables,
        grad_gains,
        offsets_early,
        offsets_late,
    ) = summed
    grad_offsets = jnp.concatenate([offsets_early, offsets_late], axis=1)
    sectioned = jnp.concatenate(
        [
            jnp.where(is_first, outputs_at[page_no], outputs_at[page_no + 1])
            for page_no in range(page_count)
        ],
        axis=0,
    )
    input_grads = jnp.concatenate(
        [
            jnp.where(is_first, grads_at[page_no], grads_at[page_no + 1])
            for page_no in range(page_count)
        ],
        axis=0,
    )
    return (
        sectioned[None],
        input_grads[None],
        grad_in,
        grad_out,
        grad_up,
        grad_down,
        grad_tables,
        grad_gains,
        grad_offsets,
        grad_hidden,
    )


def solution(mesh):
    placed = (
        P("wide", None),
        P("wide", None),
        P("wide"),
        P(None, "wide"),
        P("section", None, None),
        P("section", None, None),
        P("section", None, None),
        P("section", None, None),
        P("section", None, None, None),
        P("section", None, None),
        P("section", None, None),
        P("section", None),
    )
    return jax.shard_map(
        local,
        mesh=mesh,
        in_specs=placed,
        out_specs=(
            P("section", "wide", None),
            P("section", "wide", None),
            P("section", "wide", None),
            P("section", "wide", None),
            P("section", "wide", None),
            P("section", "wide", None),
            P("section", None, None, "wide"),
            P("section", None, "wide"),
            P("section", None, "wide"),
            P("section", "wide"),
        ),
        check_vma=False,
    )
```

profile of v0, /device:TPU:0, one launch (start us, length us, event | category | flops | bytes accessed | tf_op | source)
XLA Modules:
  0.0 1148.2 jit_solution(3111049408205981908)
XLA Ops:
  14.3 44.0 %conditional.9 = (bf16[256,768]{1,0:T(8,128)(2,1)S(1)}, bf16[256,2304]{1,0:T(8,128)(2,1)S(1)}, f32[12,256]{1,0:T(8,128)S(1)}, bf16[256,768]{0,1:T(8,128)(2,1)}, ...) conditional(s32[]{:T(128)} %convert_element_type.288, () %tuple.88, ...), branch_computations={%region_0.1_spmd, %region_1.8_spmd} | conditional | flops 4061038592 | bytes 108813096 | solution.py:251
  17.5 3.1 fusion.75
  25.3 3.0 fusion.309
  30.4 3.6 fusion.99
  40.7 4.2 convolution_add_fusion.4
  45.0 10.5 fusion.315
  62.9 6.5 collective-permute-done
  71.2 43.7 %conditional.10 = (bf16[256,768]{1,0:T(8,128)(2,1)S(1)}, bf16[256,2304]{1,0:T(8,128)(2,1)S(1)}, f32[12,256]{1,0:T(8,128)S(1)}, bf16[256,768]{0,1:T(8,128)(2,1)},...) conditional(s32[]{:T(128)} %convert_element_type.290, () %tuple.90, ...), branch_computations={%region_8.9_spmd, %region_9.16_spmd} | conditional | flops 4061038592 | bytes 108763912 | solution.py:251
  74.7 3.1 fusion.135
  82.4 3.0 fusion.317
  87.6 3.6 fusion.159
  91.2 2.4 fusion.322
  97.4 4.2 convolution_add_fusion.7
  101.6 10.6 fusion.323
  115.5 4.4 collective-permute-start.1
  124.3 4.0 collective-permute-done.1
  128.3 6.4 conditional.11
  135.9 16.8 %conditional.12 = (f32[256,768]{1,0:T(8,128)S(1)}, f32[3072,768]{1,0:T(8,128)}, f32[3072]{0:T(1024)}, f32[2,768]{1,0:T(2,128)}, f32[3,768]{1,0:T(4,128)S(1)}, /*index=5*/f32[768,3072]{1,0:T(8,128)}) conditional(s32[]{:T(128)} %convert_element_type.292, () %tuple.99, (f32[2,768]{1,0:T(2,128)}, f32[256,768]{1,0:T(8,128)}, f32[256,768]{1,0:T(8,128)}, ...), branch_computations={%region_24.25_spmd, %region_25.40_spmd} | conditional | flops 4901243904 | bytes 116547744 | solution.py:286
  143.7 4.2 broadcast.974
  148.0 4.7 broadcast.973.clone
  153.3 9.0 conditional.13
  158.9 3.3 broadcast.1013.clone
  162.3 7.1 collective-permute-start.2
  169.4 116.3 %collective-permute-done.2 = bf16[256,768]{1,0:T(8,128)(2,1)S(1)} collective-permute-done((bf16[256,768]{1,0:T(8,128)(2,1)}, bf16[256,768]{1,0:T(8,128)(2,1)S(1)}, u32[]{:S(2)}, u32[]{:S(2)}) %collective-permute-start.2) | collective-permute-done | bytes 393248 | tf_op jit(solution)/shard_map/ppermute | solution.py:16
  287.7 49.8 %conditional.14 = (f32[256,768]{1,0:T(8,128)S(1)}, f32[3072,768]{1,0:T(8,128)}, f32[3072]{0:T(1024)}, f32[2,768]{1,0:T(2,128)S(1)}, f32[3,768]{1,0:T(4,128)}, /*index=5*/f32[768,3072]{1,0:T(8,128)}) conditional(s32[]{:T(128)} %convert_element_type.290, () %tuple.97, (f32[2,768]{1,0:T(2,128)S(1)}, f32[256,768]{1,0:T(8,128)}, f32[256,768]{1,0:T(8,128)}, ...), branch_computations={%region_45.46_spmd, %region_46.61_spmd} | conditional | flops 4901243904 | bytes 116551872 | solution.py:286
  298.4 10.8 convert_reduce_fusion.8
  309.2 2.9 multiply_reduce_fusion.16
  314.4 7.5 fusion.272
  321.9 6.1 convolution_bitcast_fusion.7
  327.9 9.6 copy.214
  338.1 50.5 %conditional.15 = (f32[256,768]{1,0:T(8,128)}, f32[768,768]{1,0:T(8,128)}, f32[3,12,1024]{2,1,0:T(8,128)}, f32[3,768]{1,0:T(4,128)}, bf16[256,768]{1,0:T(8,128)(...) conditional(s32[]{:T(128)} %convert_element_type.290, () %tuple.96, (pred[256]{0:T(512)(128)(4,1)}, ...), branch_computations={%region_61.62_spmd, %region_62.0_spmd} | conditional | flops 3375462912 | bytes 102213200 | solution.py:294
  346.2 3.0 fusion.47
  353.8 5.8 multiply_reduce_fusion.1
  359.7 3.5 multiply_convert_fusion.1
  372.1 4.4 fusion.292
  376.5 4.0 convolution_bitcast_fusion.2
  380.5 8.1 copy.216
  389.9 10.2 collective-permute-done.3
  402.3 50.2 %conditional.16 = (f32[256,768]{1,0:T(8,128)S(1)}, f32[3072,768]{1,0:T(8,128)}, f32[3072]{0:T(1024)}, f32[2,768]{1,0:T(2,128)S(1)}, f32[3,768]{1,0:T(4,128)}, /*index=5*/f32[768,3072]{1,0:T(8,128)}) conditional(s32[]{:T(128)} %convert_element_type.288, () %tuple.95, (f32[2,768]{1,0:T(2,128)S(1)}, f32[256,768]{1,0:T(8,128)}, f32[256,768]{1,0:T(8,128)}, ...), branch_computations={%region_66.67_spmd, %region_67.82_spmd} | conditional | flops 4901243904 | bytes 116551872 | solution.py:286
  413.0 10.8 convert_reduce_fusion.10
  423.8 2.9 multiply_reduce_fusion.22
  429.0 7.5 fusion.283
  436.4 6.1 convolution_bitcast_fusion.8
  442.6 9.6 copy.218
  458.5 40.9 %conditional.17 = (f32[256,768]{1,0:T(8,128)}, f32[768,768]{1,0:T(8,128)}, f32[3,12,1024]{2,1,0:T(8,128)}, f32[3,768]{1,0:T(4,128)}, f32[768,2304]{1,0:T(8,128)}) conditional(s32[]{:T(128)} %convert_element_type.288, () %tuple.94, (pred[256]{0:T(512)(128)(4,1)}, bf16[256,2304]{1,0:T(8,128)(2,1)S(1)}, bf16[1,3,12,1024]{3,2,1,0:T(8,128)(2,1)}, ...), branch_computations={%region_82.83_spmd, %region_83.87_spmd} | conditional | flops 3375069696 | bytes 124097168 | solution.py:294
  465.0 3.2 fusion.72
  471.1 5.1 multiply_reduce_fusion.2
  476.3 2.5 multiply_convert_fusion.2
  487.3 4.0 convolution_bitcast_fusion.4
  491.4 8.0 copy.220
  500.1 3.1 bitcast_reduce_fusion.1
  509.6 15.7 %copy.199 = f32[1,3,12,1024]{0,2,1,3:T(8,128)} copy(f32[1,3,12,1024]{3,0,2,1:T(1,128)S(1)} %broadcast_in_dim.184) | data formatting | bytes 294912
  525.4 12.6 %bitcast_reduce_fusion = f32[1024,3,12]{2,1,0:T(4,128)S(1)} fusion(f32[1,3,12,1024]{0,2,1,3:T(8,128)} %copy.199), kind=kLoop, calls=%fused_computation.504 | loop fusion | bytes 294912
  539.6 5.2 add_bitcast_fusion.3
  544.8 11.3 add_bitcast_fusion.2
  556.2 14.8 %add_bitcast_fusion.1 = f32[1,768,3072]{2,1,0:T(8,128)} fusion(f32[768,3072]{1,0:T(8,128)} %get-tuple-element.563, f32[768,3072]{1,0:T(8,128)} %get-tuple-element.559, f32[768,3072]{1,0:T(8,128)} %get-tuple-element.561), kind=kLoop, calls=%fused_computation.506 | loop fusion | flops 4718592 | bytes 37748736 | tf_op jit(solution)/shard_map/broadcast_in_dim | solution.py:308
  571.1 13.9 %add_bitcast_fusion = f32[1,3072,768]{2,1,0:T(8,128)} fusion(f32[3072,768]{1,0:T(8,128)} %get-tuple-element.381, f32[3072,768]{1,0:T(8,128)} %get-tuple-element.379, f32[3072,768]{1,0:T(8,128)} %get-tuple-element.380), kind=kLoop, calls=%fused_computation.505 | loop fusion | flops 4718592 | bytes 37748736 | tf_op jit(solution)/shard_map/broadcast_in_dim | solution.py:309
  592.8 35.8 %reduce-scatter.32.cloned.1.call-done = f32[48,3]{1,0:T(8,128)} async-done(((f32[768,3]{1,0:T(8,128)}), f32[48,3]{1,0:T(8,128)}) %reduce-scatter.32.cloned.1.call-update) | async-done | bytes 592
  630.1 61.0 %reduce-scatter.36.cloned.1.call-done = f32[192,1]{1,0:T(8,128)} async-done(((f32[3072,1]{1,0:T(8,128)}), f32[192,1]{1,0:T(8,128)}) %reduce-scatter.36.cloned.1.call-update) | async-done | bytes 784
  692.6 56.7 %reduce-scatter.28.cloned.1.call-done = f32[64,36]{1,0:T(8,128)} async-done(((f32[1024,36]{1,0:T(8,128)}), f32[64,36]{1,0:T(8,128)}) %reduce-scatter.28.cloned.1.call-update) | async-done | bytes 9232
  751.7 64.2 %reduce-scatter.22.cloned.1.call-done = f32[1,48,768]{2,1,0:T(8,128)} async-done(((f32[1,768,768]{2,1,0:T(8,128)}), f32[1,48,768]{2,1,0:T(8,128)}) %reduce-scatter.22.cloned.1.call-update) | async-done | bytes 147472 | tf_op jit(solution)/shard_map/reduce_scatter | solution.py:307
  815.9 93.7 %reduce-scatter.20.cloned.1.call-done = f32[1,48,2304]{2,1,0:T(8,128)} async-done(((f32[1,768,2304]{2,1,0:T(8,128)}), f32[1,48,2304]{2,1,0:T(8,128)}) %reduce-scatter.20.cloned.1.call-update) | async-done | bytes 442384 | tf_op jit(solution)/shard_map/reduce_scatter | solution.py:306
  909.6 116.1 %reduce-scatter.24.cloned.1.call-done = f32[1,48,3072]{2,1,0:T(8,128)} async-done(((f32[1,768,3072]{2,1,0:T(8,128)}), f32[1,48,3072]{2,1,0:T(8,128)}) %reduce-scatter.24.cloned.1.call-update) | async-done | bytes 589840 | tf_op jit(solution)/shard_map/reduce_scatter | solution.py:308
  1025.7 115.8 %reduce-scatter.26.cloned.1.call-done = f32[1,192,768]{2,1,0:T(8,128)} async-done(((f32[1,3072,768]{2,1,0:T(8,128)}), f32[1,192,768]{2,1,0:T(8,128)}) %reduce-scatter.26.cloned.1.call-update) | async-done | bytes 589840 | tf_op jit(solution)/shard_map/reduce_scatter | solution.py:309
  (393 shorter events, 168.3 us)
Async XLA Ops:
  7.2 583.3 %reduce-scatter.30.cloned.1.call-start = ((), (), s32[]{:S(2)}) async-start(), calls=%async_computation.14 | async-start | bytes 417792
  29.9 10.7 slice-start
  30.4 4.3 copy-start.1
  30.4 4.2 copy-start.81
  30.4 10.3 slice-start.1
  34.0 4.4 copy-start.75
  34.0 4.4 copy-start.76
  34.0 6.7 copy-start.96
  38.4 6.5 slice-start.12
  40.7 4.2 copy-start.87
  40.7 4.2 slice-start.13
  44.9 12.0 %copy-start.69 = (f32[768]{0:T(1024)S(1)}, f32[768]{0:T(1024)}, u32[]{:S(2)}) copy-start(f32[768]{0:T(1024)} %get-tuple-element.565) | copy-start | bytes 9220 | tf_op jit(solution)/shard_map/cond
  44.9 12.0 %copy-start.70 = (f32[768]{0:T(1024)S(1)}, f32[768]{0:T(1024)}, u32[]{:S(2)}) copy-start(f32[768]{0:T(1024)} %get-tuple-element.661) | copy-start | bytes 9220 | tf_op jit(solution)/shard_map/cond
  44.9 13.3 %copy-start.13 = (bf16[256,2304]{1,0:T(8,128)(2,1)S(1)}, bf16[256,2304]{1,0:T(8,128)(2,1)}, u32[]{:S(2)}) copy-start(bf16[256,2304]{1,0:T(8,128)(2,1)} %copy-done.12) | copy-start | bytes 3538948 | tf_op jit(solution)/shard_map/cond
  45.0 13.3 %copy-start.62 = (f32[12,256]{1,0:T(8,128)S(1)}, f32[12,256]{1,0:T(8,128)}, u32[]{:S(2)}) copy-start(f32[12,256]{1,0:T(8,128)} %log_add_fusion) | copy-start | bytes 36868 | tf_op jit(solution)/shard_map/cond
  58.9 11.6 %copy-start.50 = (bf16[256,768]{1,0:T(8,128)(2,1)}, bf16[256,768]{1,0:T(8,128)(2,1)S(1)}, u32[]{:S(2)}) copy-start(bf16[256,768]{1,0:T(8,128)(2,1)S(1)} %get-tuple-element.336) | copy-start | bytes 1179652
  58.9 12.3 %copy-start.14 = (bf16[256,2304]{1,0:T(8,128)(2,1)}, bf16[256,2304]{1,0:T(8,128)(2,1)S(1)}, u32[]{:S(2)}) copy-start(bf16[256,2304]{1,0:T(8,128)(2,1)S(1)} %get-tuple-element.339) | copy-start | bytes 3538948
  58.9 10.5 collective-permute-start
  87.1 10.2 slice-start.2
  87.6 9.8 slice-start.3
  91.2 3.8 copy-start.77
  91.2 3.8 copy-start.78
  91.2 6.1 copy-start.97
  95.0 6.5 slice-start.14
  97.3 4.2 copy-start.88
  97.3 4.2 slice-start.15
  101.6 12.0 %copy-start.71 = (f32[768]{0:T(1024)S(1)}, f32[768]{0:T(1024)}, u32[]{:S(2)}) copy-start(f32[768]{0:T(1024)} %get-tuple-element.573) | copy-start | bytes 9220 | tf_op jit(solution)/shard_map/cond
  101.6 12.0 %copy-start.72 = (f32[768]{0:T(1024)S(1)}, f32[768]{0:T(1024)}, u32[]{:S(2)}) copy-start(f32[768]{0:T(1024)} %get-tuple-element.672) | copy-start | bytes 9220 | tf_op jit(solution)/shard_map/cond
  101.6 13.3 %copy-start.17 = (bf16[256,2304]{1,0:T(8,128)(2,1)S(1)}, bf16[256,2304]{1,0:T(8,128)(2,1)}, u32[]{:S(2)}) copy-start(bf16[256,2304]{1,0:T(8,128)(2,1)} %copy-done.16) | copy-start | bytes 3538948 | tf_op jit(solution)/shard_map/cond
  115.5 12.8 %copy-start.51 = (bf16[256,768]{1,0:T(8,128)(2,1)}, bf16[256,768]{1,0:T(8,128)(2,1)S(1)}, u32[]{:S(2)}) copy-start(bf16[256,768]{1,0:T(8,128)(2,1)S(1)} %get-tuple-element.337) | copy-start | bytes 1179652
  115.5 12.8 %copy-start.18 = (bf16[256,2304]{1,0:T(8,128)(2,1)}, bf16[256,2304]{1,0:T(8,128)(2,1)S(1)}, u32[]{:S(2)}) copy-start(bf16[256,2304]{1,0:T(8,128)(2,1)S(1)} %get-tuple-element.341) | copy-start | bytes 3538948
  115.5 12.8 %collective-permute-start.1 = (bf16[256,768]{1,0:T(8,128)(2,1)S(1)}, bf16[256,768]{1,0:T(8,128)(2,1)S(1)}, u32[]{:S(2)}, u32[]{:S(2)}) collective-permute-start(bf16[256,768]{1,0:T(8,128)(2,1)S(1)} %get-tuple-element.337), channel_id=1, source_target_pairs={{0,16},{1,17},{2,18},{3,19},{4,20},{5,21},{6,22},{7,23},{8,24},{9,... | collective-permute-start | bytes 1179656 | tf_op jit(solution)/shard_map/ppermute | solution.py:16
  135.9 17.4 %copy-start = (bf16[1,768,768]{2,1,0:T(8,128)(2,1)S(1)}, bf16[1,768,768]{2,1,0:T(8,128)(2,1)}, u32[]{:S(2)}) copy-start(bf16[1,768,768]{2,1,0:T(8,128)(2,1)} %param.35) | copy-start | bytes 3538948
  135.9 17.4 %copy-start.23 = (bf16[256,2304]{1,0:T(8,128)(2,1)S(1)}, bf16[256,2304]{1,0:T(8,128)(2,1)}, u32[]{:S(2)}) copy-start(bf16[256,2304]{1,0:T(8,128)(2,1)} %copy-done.22) | copy-start | bytes 3538948
  153.3 134.4 %copy-start.61 = (f32[1,2,768]{2,1,0:T(2,128)S(1)}, f32[1,2,768]{2,1,0:T(2,128)}, u32[]{:S(2)}) copy-start(f32[1,2,768]{2,1,0:T(2,128)} %param.39) | copy-start | bytes 18436
  162.3 123.4 %collective-permute-start.2 = (bf16[256,768]{1,0:T(8,128)(2,1)}, bf16[256,768]{1,0:T(8,128)(2,1)S(1)}, u32[]{:S(2)}, u32[]{:S(2)}) collective-permute-start(bf16[256,768]{1,0:T(8,128)(2,1)} %get-tuple-element.351), channel_id=1, source_target_pairs={{16,0},{17,1},{18,2},{19,3},{20,4},{21,5},{22,6},{23,7},{24,8},{25... | collective-permute-start | bytes 1179656 | tf_op jit(solution)/shard_map/ppermute | solution.py:16
  287.7 49.8 %copy-start.19 = (bf16[256,2304]{1,0:T(8,128)(2,1)S(1)}, bf16[256,2304]{1,0:T(8,128)(2,1)}, u32[]{:S(2)}) copy-start(bf16[256,2304]{1,0:T(8,128)(2,1)} %copy-done.18) | copy-start | bytes 3538948
  287.7 49.8 %copy-start.30 = (bf16[256,768]{1,0:T(8,128)(2,1)S(1)}, bf16[256,768]{1,0:T(8,128)(2,1)}, u32[]{:S(2)}) copy-start(bf16[256,768]{1,0:T(8,128)(2,1)} %copy-done.29) | copy-start | bytes 1179652
  287.7 9.0 copy-start.25
  292.9 5.5 copy-start.93
  298.2 11.0 slice-start.8
  298.4 10.8 slice-start.9
  344.8 4.4 copy-start.41
  346.2 5.4 copy-start.33
  349.2 4.6 copy-start.90
  359.7 3.8 copy-start.42
  388.6 11.4 collective-permute-start.3
  402.3 56.1 %copy-start.15 = (bf16[256,2304]{1,0:T(8,128)(2,1)S(1)}, bf16[256,2304]{1,0:T(8,128)(2,1)}, u32[]{:S(2)}) copy-start(bf16[256,2304]{1,0:T(8,128)(2,1)} %copy-done.14) | copy-start | bytes 3538948
  402.3 56.1 %copy-start.28 = (bf16[256,768]{1,0:T(8,128)(2,1)S(1)}, bf16[256,768]{1,0:T(8,128)(2,1)}, u32[]{:S(2)}) copy-start(bf16[256,768]{1,0:T(8,128)(2,1)} %copy-done.27) | copy-start | bytes 1179652
  402.3 9.0 copy-start.26
  407.5 5.5 copy-start.94
  412.8 11.0 slice-start.10
  413.0 10.8 slice-start.11
  456.9 134.9 %reduce-scatter.34.cloned.1.call-start = ((), (), s32[]{:S(2)}) async-start(), calls=%async_computation.16 | async-start | bytes 417792
  458.5 6.5 copy-start.10
  464.9 3.8 copy-start.35
  464.9 3.8 copy-start.37
  504.0 124.5 %reduce-scatter.32.cloned.1.call-start = ((), (), s32[]{:S(2)}) async-start(), calls=%async_computation.15 | async-start | bytes 417792
  505.9 185.2 %reduce-scatter.36.cloned.1.call-start = ((), (), s32[]{:S(2)}) async-start(), calls=%async_computation.17 | async-start | bytes 1671168
  525.3 224.0 %reduce-scatter.28.cloned.1.call-start = ((), (), s32[]{:S(2)}) async-start(), calls=%async_computation.13 | async-start | bytes 557056
  539.5 276.4 %reduce-scatter.22.cloned.1.call-start = ((), (), s32[]{:S(2)}) async-start(), calls=%async_computation.10 | async-start | bytes 2506752 | tf_op jit(solution)/shard_map/reduce_scatter | solution.py:307
  544.8 364.8 %reduce-scatter.20.cloned.1.call-start = ((), (), s32[]{:S(2)}) async-start(), calls=%async_computation.9 | async-start | bytes 7520256 | tf_op jit(solution)/shard_map/reduce_scatter | solution.py:306
  556.1 469.6 %reduce-scatter.24.cloned.1.call-start = ((), (), s32[]{:S(2)}) async-start(), calls=%async_computation.11 | async-start | bytes 10027008 | tf_op jit(solution)/shard_map/reduce_scatter | solution.py:308
  571.0 570.5 %reduce-scatter.26.cloned.1.call-start = ((), (), s32[]{:S(2)}) async-start(), calls=%async_computation.12 | async-start | bytes 10027008 | tf_op jit(solution)/shard_map/reduce_scatter | solution.py:309
  (37 other events, 61.1 us)
Sparse Core Ops, SparseCore 0:
  457.0 54.7 reduce-scatter.29
  515.7 54.5 reduce-scatter.33
  573.9 54.6 reduce-scatter.31
  632.5 58.5 reduce-scatter.35
  694.5 54.7 reduce-scatter.27
  753.9 61.9 reduce-scatter.21
  820.5 89.0 reduce-scatter.19
  914.9 110.8 reduce-scatter.23
  1030.4 111.0 reduce-scatter.25
where the time goes:
time: 1160 us; the launch traced here: 1150 us
  waiting for transfers between devices  680 us (59%)
  matrix products  161 us (14%)
  local copies, waits for them, and re-layouts  153 us (13%)
  other arithmetic  117 us (10%)
  starting transfers between devices  14.8 us (1%)
  between operations  14.3 us (1%)
    unnamed x14, waiting for transfers between devices  154 us
    ppermute x4, waiting for transfers between devices, from_behind(): lax.ppermute(value, axis, [(source, source + steps) for source in range(i...  137 us
    reduce_scatter x1, waiting for transfers between devices, local(): lax.psum_scatter(totals_ffn[0][None], 'wide', scatter_dimension=1, tiled=...  116 us
    reduce_scatter x1, waiting for transfers between devices, local(): lax.psum_scatter(totals_ffn[1][None], 'wide', scatter_dimension=1, tiled=...  116 us
    reduce_scatter x1, waiting for transfers between devices, local(): lax.psum_scatter(totals_attn[0][None], 'wide', scatter_dimension=1, tiled...  93.7 us
    reduce_scatter x1, waiting for transfers between devices, local(): lax.psum_scatter(totals_attn[1][None], 'wide', scatter_dimension=1, tiled...  64.2 us
    unnamed x64, local copies, waits for them, and re-layouts  54.8 us
    dot_general x8, matrix products, contract_rows(): lax.dot_general(left, right, (((0,), (0,)), ((), ())), preferred_element_...  41.4 us
  transfers between devices with their start and end apart: 13, of which 11 were waited for; matrix products, arithmetic and copies ran while one was open for 13% of the time, Pallas kernels for 0%

commit v1 on v0

v1 whole, which is shorter than its diff:
```python
import functools

import jax
import jax.numpy as jnp
from jax import lax
from jax.experimental import pallas as pl
from jax.experimental.pallas import tpu as pltpu
from jax.sharding import PartitionSpec as P

MESH = pl.DeviceIdType.MESH
BUCKETS = 32
LANES = 128
epsilon = 1e-05
masked_score = -1000000000.0
low = jnp.bfloat16
high = jnp.float32


def dot_nn(left, right):
    return jnp.dot(left, right, preferred_element_type=high)


def dot_nt(left, right):
    return lax.dot_general(left, right, (((1,), (1,)), ((), ())), preferred_element_type=high)


def normal_terms(values):
    below = 0.5 + 0.5 * lax.erf(values * 0.7071067811865476)
    return below, values * (0.3989422804014327 * jnp.exp(-0.5 * values * values))


def norm_rows(values):
    centered = values - jnp.mean(values, axis=-1, keepdims=True)
    spread = jnp.mean(centered * centered, axis=-1, keepdims=True)
    scale = lax.rsqrt(spread + epsilon)
    return centered * scale, scale


def norm_back(upstream, gain, normal, scale):
    scaled = upstream * gain
    middle = jnp.mean(scaled, axis=-1, keepdims=True)
    along = jnp.mean(scaled * normal, axis=-1, keepdims=True)
    return scale * (scaled - middle - normal * along)


def column_sum(values):
    return jnp.sum(values.astype(high), axis=0, keepdims=True)


def main_kernel(
    sizes,
    lengths, tokens, cotangent, onehot, spread, gains, offsets, bias,
    in_hbm, out_hbm, up_hbm, down_hbm,
    result, input_grads, left_hbm, right_hbm, tables, vectors, bias_grad,
    w_in, w_out, w_up, w_down, arrive, arrive_grad, sent_grad,
    qkv, chance, context, normal_one, scale_one, normed, normed_low, slope, hidden,
    normal_two, scale_two, picked, work, square, square_low, left, d_proj, d_att, d_before, d_branch,
    turned, turned_grad, back, d_context, d_first,
    load_sem, page_sem, left_sem, right_sem, send_sem, recv_sem,
):
    rows, width, heads, ff, pages = sizes
    size = width // heads
    pairs = heads // 2
    section = lax.axis_index("section")
    first = section == 0
    block = 64
    chunk = 512

    def peer_copy(src, dst, slot):
        return pltpu.make_async_remote_copy(
            src_ref=src, dst_ref=dst, send_sem=send_sem.at[slot], recv_sem=recv_sem.at[slot],
            device_id={"section": 1 - section}, device_id_type=MESH)

    def page_rows(page):
        return pl.ds(pl.multiple_of(page * rows, rows), rows)

    loads = [pltpu.make_async_copy(src, dst, load_sem.at[at]) for at, (src, dst) in enumerate(
        ((in_hbm, w_in), (out_hbm, w_out), (up_hbm, w_up), (down_hbm, w_down)))]

    def own_copy(page):
        return pltpu.make_async_copy(tokens.at[page_rows(page)], arrive.at[page], page_sem.at[page])

    def own_grad_copy(page):
        return pltpu.make_async_copy(cotangent.at[page_rows(page)], arrive_grad.at[page], page_sem.at[page])

    @pl.when(first)
    def _():
        for page in range(pages):
            own_copy(page).start()

    for load in loads:
        load.start()

    @pl.when(section == 1)
    def _():
        for page in range(pages):
            own_grad_copy(page).start()

    barrier = pltpu.get_barrier_semaphore()
    pl.semaphore_signal(barrier, inc=1, device_id={"section": 1 - section}, device_id_type=MESH)
    pl.semaphore_wait(barrier, 1)

    tables[...] = jnp.zeros_like(tables)
    vectors[...] = jnp.zeros_like(vectors)
    bias_grad[...] = jnp.zeros_like(bias_grad)

    def left_copy(page):
        return pltpu.make_async_copy(
            left, left_hbm.at[:, pl.ds(pl.multiple_of(page * rows, rows), rows)], left_sem)

    def right_copies(page):
        found, at = [], 0
        for slot, piece in enumerate((d_proj, d_att, d_before, d_branch)):
            cols = piece.shape[1]
            found.append(pltpu.make_async_copy(
                piece, right_hbm.at[page_rows(page), pl.ds(at, cols)], right_sem.at[slot]))
            at += cols
        return found

    lane = lax.broadcasted_iota(jnp.int32, (rows, LANES), 1)
    side = lane < size

    def result_copy(page):
        return peer_copy(result.at[page_rows(page)], arrive.at[page], page)

    def grad_copy(page):
        return peer_copy(sent_grad.at[page], arrive_grad.at[page], pages + page)

    def forward(page, carry):
        @pl.when(first)
        def _():
            own_copy(page).wait()

        @pl.when(section == 1)
        def _():
            result_copy(page).wait_recv()

        @pl.when(page == 0)
        def _():
            loads[0].wait()

        @pl.when(page > 0)
        def _():
            left_copy(page - 1).wait()

        layer_in = arrive[page]
        for part in range(3):
            cols = slice(part * width, (part + 1) * width)
            found = dot_nn(layer_in, w_in[:, cols])
            if part != 1:
                found = found + offsets[part // 2 : part // 2 + 1, :]
            qkv[page, :, cols] = found.astype(low)
        left[0:width, :] = layer_in.T
        mark = onehot[page_rows(page), :]
        picked[...] = dot_nn(mark, spread[...]).astype(low)
        live = lax.broadcasted_iota(jnp.int32, (1, rows), 1) < lengths[page]
        zero = jnp.zeros((rows, LANES), low)
        for pair in range(pairs):
            cols = slice(pair * LANES, (pair + 1) * LANES)
            query = qkv[page, :, cols] * jnp.asarray(size**-0.5, low)
            keyed = jnp.concatenate([qkv[page, :, width + pair * LANES : width + (pair + 1) * LANES], mark], axis=1)
            valued = qkv[page, :, 2 * width + pair * LANES : 2 * width + (pair + 1) * LANES]
            found = []
            for half in range(2):
                head = 2 * pair + half
                mine = jnp.where(side if half == 0 else ~side, query, zero)
                full = jnp.concatenate([mine, picked[:, head * LANES : (head + 1) * LANES]], axis=1)
                square[half] = dot_nt(full, keyed)
            for half in range(2):
                head = 2 * pair + half
                for at in range(0, rows, block):
                    scores = jnp.where(live, square[half, at : at + block], masked_score)
                    raised = jnp.exp(scores - jnp.max(scores, axis=-1, keepdims=True))
                    share = raised * (1.0 / jnp.sum(raised, axis=-1, keepdims=True))
                    chance[page, head, at : at + block] = share
                    square_low[half, at : at + block] = share.astype(low)
            for half in range(2):
                found.append(dot_nn(square_low[half], valued))
            context[:, cols] = jnp.where(side, found[0], found[1]).astype(low)
        left[width : 2 * width, :] = context[...].T

        @pl.when(page == 0)
        def _():
            loads[1].wait()

        work[...] = dot_nn(context[...], w_out[...])
        for at in range(0, rows, block):
            here = slice(at, at + block)
            summed = arrive[page, here].astype(high) + (work[here] + offsets[2:3])
            normal, scale = norm_rows(summed)
            normal_one[page, here] = normal
            scale_one[page, here] = scale
            shifted = normal * gains[0:1] + offsets[3:4]
            normed[here] = shifted
            normed_low[here] = shifted.astype(low)
        left[2 * width : 3 * width, :] = normed_low[...].T

        @pl.when(page == 0)
        def _():
            loads[2].wait()
            loads[3].wait()

        for at in range(0, ff, chunk):
            cols = slice(at, at + chunk)
            before = dot_nn(normed_low[...], w_up[:, cols]) + bias[:, cols]
            below, density = normal_terms(before)
            hidden[:, cols] = (before * below).astype(low)
            slope[page, :, cols] = (below + density).astype(slope.dtype)
        share = width // 16
        deep = ff // width
        spun = hidden[...].T
        for at in range(16):
            for part in range(deep):
                left[3 * width + part * width + at * share : 3 * width + part * width + (at + 1) * share] = (
                    spun[(at * deep + part) * share : (at * deep + part + 1) * share])
        work[...] = dot_nn(hidden[...], w_down[...])
        for at in range(0, rows, block):
            here = slice(at, at + block)
            normal, scale = norm_rows(normed[here] + (work[here] + offsets[4:5]))
            normal_two[page, here] = normal
            scale_two[page, here] = scale
            result[pl.ds(pl.multiple_of(page * rows + at, block), block), :] = (
                normal * gains[1:2] + offsets[5:6]).astype(low)

        @pl.when(first)
        def _():
            result_copy(page).start()

        left_copy(page).start()
        return carry

    lax.fori_loop(0, pages, forward, 0)

    def backward(page, carry):
        @pl.when(first)
        def _():
            grad_copy(page).wait_recv()

        @pl.when(section == 1)
        def _():
            own_grad_copy(page).wait()

        @pl.when(page > 0)
        def _():
            for copy in right_copies(page - 1):
                copy.wait()

        sums = [jnp.zeros((1, width), high) for _ in range(8)]
        for at in range(0, rows, block):
            here = slice(at, at + block)
            upstream = arrive_grad[page, here].astype(high)
            normal = normal_two[page, here]
            sums[1] += column_sum(upstream * normal)
            sums[7] += column_sum(upstream)
            d_second = norm_back(upstream, gains[1:2], normal, scale_two[page, here])
            d_first[here] = d_second
            branch = d_second.astype(low)
            sums[6] += column_sum(branch)
            d_branch[here] = branch
        for at in range(0, ff, chunk):
            cols = slice(at, at + chunk)
            d_hidden = dot_nt(d_branch[...], w_down[cols, :])
            d_chunk = (d_hidden * slope[page, :, cols].astype(high)).astype(low)
            d_before[:, cols] = d_chunk
            bias_grad[:, cols] += column_sum(d_chunk)
        work[...] = dot_nt(d_before[...], w_up[...])
        for at in range(0, rows, block):
            here = slice(at, at + block)
            d_normed = d_first[here] + work[here]
            normal = normal_one[page, here]
            sums[0] += column_sum(d_normed * normal)
            sums[5] += column_sum(d_normed)
            found = norm_back(d_normed, gains[0:1], normal, scale_one[page, here])
            d_first[here] = found
            attended = found.astype(low)
            sums[4] += column_sum(attended)
            d_att[here] = attended
        d_context[...] = dot_nt(d_att[...], w_out[...]).astype(low)
        turned[...] = qkv[page, :, 0:width].T
        turned_grad[...] = d_context[...].T
        mark = onehot[page_rows(page), :]
        mark_turned = mark.T
        zero = jnp.zeros((rows, LANES), low)
        scaling = size**-0.5
        for pair in range(pairs):
            cols = slice(pair * LANES, (pair + 1) * LANES)
            keyed = jnp.concatenate([qkv[page, :, width + pair * LANES : width + (pair + 1) * LANES], mark], axis=1)
            valued = qkv[page, :, 2 * width + pair * LANES : 2 * width + (pair + 1) * LANES]
            given = d_context[:, cols]
            for half in range(2):
                mine = jnp.where(side if half == 0 else ~side, given, zero)
                square[half] = dot_nt(mine, valued)
            found = []
            for half in range(2):
                head = 2 * pair + half
                for at in range(0, rows, block):
                    share = chance[page, head, at : at + block]
                    both = share * square[half, at : at + block]
                    d_scores = both - share * jnp.sum(both, axis=-1, keepdims=True)
                    square_low[half, at : at + block] = d_scores.astype(low)
            for half in range(2):
                head = 2 * pair + half
                slim = slice(head * size, (head + 1) * size)
                both = dot_nn(square_low[half], keyed)
                found.append(both[:, :LANES])
                rest = both[:, LANES:]
                upper = rest.astype(low)
                lower = (rest - upper.astype(high)).astype(low)
                crossed = dot_nn(mark_turned, jnp.concatenate([upper, lower], axis=1))
                crossed = crossed[:, :LANES] + crossed[:, LANES:]
                place = lax.broadcasted_iota(jnp.int32, (BUCKETS, LANES), 1)
                tables[head] += jnp.where(
                    place < BUCKETS, crossed[:BUCKETS],
                    jnp.where(place < 2 * BUCKETS, crossed[BUCKETS : 2 * BUCKETS], crossed[2 * BUCKETS : 3 * BUCKETS]))
                back[slim, :] = dot_nn(turned[slim, :], square_low[half]) * scaling
                back[slice(width + head * size, width + (head + 1) * size), :] = dot_nn(
                    turned_grad[slim, :], chance[page, head].astype(low))
            d_proj[:, cols] = (jnp.where(side, found[0], found[1]) * scaling).astype(low)
        d_proj[:, width:] = back[...].astype(low).T
        sums[2] += column_sum(d_proj[:, 0:width])
        sums[3] += column_sum(d_proj[:, 2 * width :])
        for row, value in enumerate(sums):
            vectors[row : row + 1, :] += value
        work[...] = dot_nt(d_proj[...], w_in[...])
        for at in range(0, rows, block):
            here = slice(at, at + block)
            d_in = d_first[here] + work[here]
            narrow = d_in.astype(low)
            sent_grad[page, here] = narrow
            input_grads[pl.ds(pl.multiple_of(page * rows + at, block), block), :] = jnp.where(
                first, d_in, narrow.astype(high))

        @pl.when(section == 1)
        def _():
            grad_copy(page).start()

        for copy in right_copies(page):
            copy.start()
        return carry

    lax.fori_loop(0, pages, backward, 0)
    left_copy(pages - 1).wait()
    for copy in right_copies(pages - 1):
        copy.wait()
    for page in range(pages):
        @pl.when(first)
        def _():
            result_copy(page).wait_send()

        @pl.when(section == 1)
        def _():
            grad_copy(page).wait_send()


def both_passes(tokens, cotangent, lengths, onehot, spread, params):
    in_proj, out_proj, up_proj, down_proj, gains, offsets, bias, heads = params
    pages = lengths.shape[0]
    rows = tokens.shape[0] // pages
    width, ff = up_proj.shape
    sizes = (rows, width, heads, ff, pages)
    VM = pltpu.VMEM
    here, there = pl.BlockSpec(memory_space=pltpu.VMEM), pl.BlockSpec(memory_space=pl.ANY)
    scratch = [
        VM(in_proj.shape, low), VM(out_proj.shape, low), VM(up_proj.shape, low), VM(down_proj.shape, low),
        VM((pages, rows, width), low), VM((pages, rows, width), low), VM((pages, rows, width), low),
        VM((pages, rows, 3 * width), low),
        VM((pages, heads, rows, rows), high),
        VM((rows, width), low),
        VM((pages, rows, width), high), VM((pages, rows, 1), high),
        VM((rows, width), high), VM((rows, width), low),
        VM((pages, rows, ff), high),
        VM((rows, ff), low),
        VM((pages, rows, width), high), VM((pages, rows, 1), high),
        VM((rows, heads * LANES), low),
        VM((rows, width), high),
        VM((2, rows, rows), high), VM((2, rows, rows), low),
        VM((3 * width + ff, rows), low),
        VM((rows, 3 * width), low), VM((rows, width), low), VM((rows, ff), low), VM((rows, width), low),
        VM((width, rows), low), VM((width, rows), low), VM((2 * width, rows), high),
        VM((rows, width), low), VM((rows, width), high),
        pltpu.SemaphoreType.DMA((4,)), pltpu.SemaphoreType.DMA((pages,)), pltpu.SemaphoreType.DMA,
        pltpu.SemaphoreType.DMA((4,)), pltpu.SemaphoreType.DMA((2 * pages,)), pltpu.SemaphoreType.DMA((2 * pages,)),
    ]
    return pl.pallas_call(
        functools.partial(main_kernel, sizes),
        out_shape=(
            jax.ShapeDtypeStruct(tokens.shape, low),
            jax.ShapeDtypeStruct(tokens.shape, high),
            jax.ShapeDtypeStruct((3 * width + ff, pages * rows), low),
            jax.ShapeDtypeStruct((pages * rows, 5 * width + ff), low),
            jax.ShapeDtypeStruct((heads, BUCKETS, LANES), high),
            jax.ShapeDtypeStruct((8, width), high),
            jax.ShapeDtypeStruct((1, ff), high),
        ),
        in_specs=[pl.BlockSpec(memory_space=pltpu.SMEM), there, there, here, here, here, here, here] + [there] * 4,
        out_specs=(here, here, there, there, here, here, here),
        scratch_shapes=scratch,
        compiler_params=pltpu.CompilerParams(
            collective_id=0, has_side_effects=True, vmem_limit_bytes=63 * 2**20),
    )(lengths, tokens, cotangent, onehot, spread, gains, offsets, bias[None], in_proj, out_proj, up_proj, down_proj)


def marks_of(buckets):
    levels = jnp.arange(LANES, dtype=jnp.int32)
    own = jnp.where(levels < BUCKETS, buckets[0][:, None], jnp.where(levels < 2 * BUCKETS, buckets[1][:, None], buckets[2][:, None]))
    return jnp.logical_and(own == levels % BUCKETS, levels < 3 * BUCKETS).astype(low)


def spread_of(layout):
    axes, heads, _ = layout.shape
    grid = layout.reshape(axes, heads, BUCKETS, BUCKETS)
    placed = [
        jnp.pad(grid[a].transpose(1, 0, 2), ((0, 0), (0, 0), (a * BUCKETS, LANES - (a + 1) * BUCKETS)))
        for a in range(axes)
    ]
    placed.append(jnp.zeros_like(placed[0]))
    return jnp.concatenate(placed, axis=0).reshape(LANES, heads * LANES)


LAGS = (0, 1, 7, 10, 13)


def left_of(at):
    return jnp.where(at < 9, 0, jnp.where(at < 12, 1, jnp.where(at < 24, 2, 3 + (at - 24) // 3)))


def right_of(at):
    return jnp.where(at < 24, at, 24 + at % 3)


def rs_kernel(
    count, levels, rows, cols, lags, compute,
    xt_ref, dy_ref, small_ref, out_ref, small_out_ref,
    dw, k1, k2, k3, s0, s1, s2, s3, r0, r1, r2, r3, ssem, rsem,
    ks0, ks1, ks2, ss0, ss1, ss2, ss3, sr0, sr1, sr2, sr3, sssem, srsem,
):
    me = lax.axis_index("wide")
    keeps, sends, recvs = (dw, k1, k2, k3), (s0, s1, s2, s3), (r0, r1, r2, r3)
    skeeps, ssends, srecvs = (small_ref, ks0, ks1, ks2), (ss0, ss1, ss2, ss3), (sr0, sr1, sr2, sr3)
    bits = [(me // 2**level) % 2 for level in range(levels)]
    partners = [me + 2**level * (1 - 2 * bits[level]) for level in range(levels)]

    barrier = pltpu.get_barrier_semaphore()
    for partner in partners:
        pl.semaphore_signal(barrier, inc=1, device_id={"wide": partner}, device_id_type=MESH)
    pl.semaphore_wait(barrier, levels)

    def copy(level, at):
        return pltpu.make_async_remote_copy(
            src_ref=sends[level].at[at], dst_ref=recvs[level].at[at],
            send_sem=ssem.at[level, at], recv_sem=rsem.at[level, at],
            device_id={"wide": partners[level]}, device_id_type=MESH)

    def small_copy(level):
        return pltpu.make_async_remote_copy(
            src_ref=ssends[level], dst_ref=srecvs[level],
            send_sem=sssem.at[level], recv_sem=srsem.at[level],
            device_id={"wide": partners[level]}, device_id_type=MESH)

    def start(at):
        slot = at % keeps[0].shape[0]
        if compute:
            dw[slot] = jnp.dot(xt_ref[left_of(at)], dy_ref[right_of(at)],
                               preferred_element_type=jnp.float32).reshape(dw.shape[1:])
        half = 2 ** (levels - 1)
        for j in range(half):
            s0[at, j] = dw[slot, 2 * j + 1 - bits[0]].astype(s0.dtype)
        copy(0, at).start()

    def middle(level, at):
        copy(level - 1, at).wait_recv()
        half = 2 ** (levels - 1 - level)
        old = at % keeps[level - 1].shape[0]
        new = at % keeps[level].shape[0]
        before = bits[level - 1]
        for j in range(half):
            pick = 2 * j + 1 - bits[level]
            total = keeps[level - 1][old, 2 * pick + before] if level == 1 else keeps[level - 1][old, pick]
            sends[level][at, j] = (total + recvs[level - 1][at, pick].astype(jnp.float32)).astype(sends[level].dtype)
        copy(level, at).start()
        for j in range(half):
            pick = 2 * j + bits[level]
            total = keeps[level - 1][old, 2 * pick + before] if level == 1 else keeps[level - 1][old, pick]
            keeps[level][new, j] = total + recvs[level - 1][at, pick].astype(jnp.float32)

    def finish(at):
        copy(levels - 1, at).wait_recv()
        old = at % keeps[levels - 1].shape[0]
        columns = pl.ds(pl.multiple_of(at * cols, cols), cols)
        out_ref[:, columns] = keeps[levels - 1][old, 0] + recvs[levels - 1][at, 0].astype(jnp.float32)

    def small_stage(level):
        if level:
            small_copy(level - 1).wait_recv()
        if level == levels:
            small_out_ref[...] = skeeps[levels - 1][0] + srecvs[levels - 1][0]
            return
        half = 2 ** (levels - 1 - level)
        for kept in (0, 1):
            for j in range(half):
                pick = 2 * j + (bits[level] if kept else 1 - bits[level])
                if level == 0:
                    value = small_ref[pick]
                else:
                    at = 2 * pick + bits[0] if level == 1 else pick
                    value = skeeps[level - 1][at] + srecvs[level - 1][pick]
                if not kept:
                    ssends[level][j] = value
                elif level:
                    skeeps[level][j] = value
            if not kept:
                small_copy(level).start()

    def step(moment, carry):
        for level in range(levels + 1):
            due = moment - lags[level]

            @pl.when(jnp.logical_and(due >= 0, due < count))
            def _():
                at = count - 1 - due
                if level == 0:
                    start(at)
                elif level < levels:
                    middle(level, at)
                else:
                    finish(at)
        return carry

    lax.fori_loop(0, count // 2, step, 0)
    small_stage(0)
    small_stage(1)
    lax.fori_loop(count // 2, count, step, 0)
    small_stage(2)
    small_stage(3)
    small_stage(4)
    lax.fori_loop(count, count + lags[levels], step, 0)

    def drain(at, carry):
        for level in range(levels):
            copy(level, at).wait_send()
        return carry

    lax.fori_loop(0, count, drain, 0)
    for level in range(levels):
        small_copy(level).wait_send()


def reduce_grads(xt, dy, small, lags=LAGS, compute=True, count=36, levels=4, wire=jnp.bfloat16, cid=1):
    n = 2**levels
    deep = dy.shape[0]
    cols = dy.shape[1] // 27
    rows = 3 * cols // n
    xt = xt.reshape(7, 3 * cols, deep)
    dy = dy.reshape(deep, 27, cols).transpose(1, 0, 2)
    def ring(level):
        return lags[level + 1] - lags[level] + 1
    VM = pltpu.VMEM
    scratch = [VM((ring(0), n, rows, cols), jnp.float32)]
    scratch += [VM((ring(l), n >> (l + 1), rows, cols), jnp.float32) for l in (1, 2, 3)]
    scratch += [VM((count, n >> (l + 1), rows, cols), wire) for l in range(4)]
    scratch += [VM((count, n >> (l + 1), rows, cols), wire) for l in range(4)]
    scratch += [pltpu.SemaphoreType.DMA((levels, count))] * 2
    sm = small.shape[1:]
    scratch += [VM((n >> (l + 1),) + sm, jnp.float32) for l in (1, 2, 3)]
    scratch += [VM((n >> (l + 1),) + sm, jnp.float32) for l in range(4)] * 2
    scratch += [pltpu.SemaphoreType.DMA((levels,))] * 2
    return pl.pallas_call(
        functools.partial(rs_kernel, count, levels, rows, cols, lags, compute),
        out_shape=(jax.ShapeDtypeStruct((rows, count * cols), jnp.float32),
                   jax.ShapeDtypeStruct(sm, jnp.float32)),
        in_specs=[pl.BlockSpec(memory_space=pltpu.VMEM)] * 3,
        out_specs=(pl.BlockSpec(memory_space=pltpu.VMEM),) * 2,
        scratch_shapes=scratch,
        compiler_params=pltpu.CompilerParams(collective_id=cid, has_side_effects=True, vmem_limit_bytes=63 * 2**20),
    )(xt, dy, small)


def local(tokens, cotangent, lengths, buckets, in_proj, out_proj, up_proj, down_proj, layout_tables, norm_gains, offsets, hidden_bias):
    heads = layout_tables.shape[2]
    width, ff = up_proj.shape[1:]
    params = (in_proj[0], out_proj[0], up_proj[0], down_proj[0], norm_gains[0], offsets[0], hidden_bias[0], heads)
    result, input_grads, left, right, tables, vectors, bias_grad = both_passes(
        tokens, cotangent, lengths, marks_of(buckets), spread_of(layout_tables[0]), params)
    wide_count = lax.axis_size("wide")
    share, deep = width // wide_count, ff // width
    tables = tables[:, :, : 3 * BUCKETS].reshape(heads, BUCKETS, 3, BUCKETS).transpose(2, 0, 1, 3).reshape(3 * heads, -1)
    if wide_count == 16 and share % 16 == 0:
        small = jnp.concatenate(
            [
                tables.reshape(3 * heads, wide_count, -1).transpose(1, 0, 2).reshape(wide_count, -1),
                vectors.reshape(8, wide_count, -1).transpose(1, 0, 2).reshape(wide_count, -1),
                bias_grad.reshape(wide_count, -1),
            ],
            axis=1,
        )
        filled = small.shape[1]
        small = jnp.pad(small, ((0, 0), (0, -filled % 1024))).reshape(wide_count, -1, 128)
        grads, few = reduce_grads(left, right, small)
        few = few.reshape(-1)
        tables_size = 3 * heads * BUCKETS * BUCKETS // wide_count
        grad_tables = few[:tables_size].reshape(1, 3, heads, -1)
        vectors = few[tables_size : tables_size + 8 * share].reshape(1, 8, share)
        grad_hidden = few[tables_size + 8 * share : filled].reshape(1, -1)
        grad_in = grads[None, :, : 3 * width]
        grad_out = grads[None, :, 3 * width : 4 * width]
        grad_up = grads[None, :, 4 * width : 4 * width + ff]
        grad_down = grads[:, 4 * width + ff :].reshape(share, deep, width)
        grad_down = grad_down.transpose(1, 0, 2).reshape(1, deep * share, width)
    else:

        def scattered(value, dim):
            return lax.psum_scatter(value[None], "wide", scatter_dimension=dim, tiled=True)

        def product(rows_from, cols_from, cols):
            return dot_nn(left[rows_from : rows_from + width], right[:, cols_from : cols_from + cols])

        slim = width // 16
        grad_in = scattered(product(0, 0, 3 * width), 1)
        grad_out = scattered(product(width, 3 * width, width), 1)
        grad_up = scattered(product(2 * width, 4 * width, ff), 1)
        grad_down = dot_nn(left[3 * width :], right[:, 4 * width + ff :])
        grad_down = grad_down.reshape(deep, 16, slim, width).transpose(1, 0, 2, 3).reshape(ff, width)
        grad_down = scattered(grad_down, 1)
        grad_hidden = scattered(bias_grad[0], 1)
        grad_tables = scattered(tables.reshape(3, heads, -1), 3)
        vectors = scattered(vectors, 2)
    return (
        result[None],
        input_grads[None],
        grad_in,
        grad_out,
        grad_up,
        grad_down,
        grad_tables,
        vectors[:, :2],
        vectors[:, 2:],
        grad_hidden,
    )


def solution(mesh):
    placed = (
        P("wide", None),
        P("wide", None),
        P("wide"),
        P(None, "wide"),
        P("section", None, None),
        P("section", None, None),
        P("section", None, None),
        P("section", None, None),
        P("section", None, None, None),
        P("section", None, None),
        P("section", None, None),
        P("section", None),
    )
    return jax.shard_map(
        local,
        mesh=mesh,
        in_specs=placed,
        out_specs=(
            P("section", "wide", None),
            P("section", "wide", None),
            P("section", "wide", None),
            P("section", "wide", None),
            P("section", "wide", None),
            P("section", "wide", None),
            P("section", None, None, "wide"),
            P("section", None, "wide"),
            P("section", None, "wide"),
            P("section", "wide"),
        ),
        check_vma=False,
    )
```

time: 1160 us -> 236 us (0.20)
  waiting for transfers between devices: 680 us -> 0 us
  Pallas kernels: 0 us -> 190 us
  matrix products: 161 us -> 0 us
  other arithmetic: 117 us -> 2.49 us
  local copies, waits for them, and re-layouts: 153 us -> 42.3 us
  starting transfers between devices: 14.8 us -> 0 us
  between operations: 14.3 us -> 0.79 us
    reduce_scatter x4 -> x0, waiting for transfers between devices: 390 us -> none  [the longest x1 116 us: local(): lax.psum_scatter(totals_ffn[0][None], 'wide', scatter_dimension=1, tiled=...]
    pallas_call x0 -> x2, Pallas kernels: none -> 190 us  [the longest x1 102 us: reduce_grads(): pl.pallas_call(functools.partial(rs_kernel, count, levels, rows, cols, la...]
    dot_general x46 -> x0, matrix products: 161 us -> none  [the longest x8 41.4 us: contract_rows(): lax.dot_general(left, right, (((0,), (0,)), ((), ())), preferred_element_...]
    unnamed x14 -> x0, waiting for transfers between devices: 154 us -> none
    ppermute x4 -> x0, waiting for transfers between devices: 137 us -> none  [from_behind(): lax.ppermute(value, axis, [(source, source + steps) for source in range(i...]
    unnamed x64 -> x8, local copies, waits for them, and re-layouts: 54.8 us -> 4.08 us
    broadcast_in_dim x7 -> x0, other arithmetic: 48.7 us -> none  [the longest x1 14.8 us: local(): totals_ffn[0][None]]
    cond x134 -> x0, local copies, waits for them, and re-layouts: 43.8 us -> none  [the longest x2 19.2 us: local(): lax.cond(usable, lambda: ffn_backward(stored_all[moment], params, upstrea...]
  transfers between devices with their start and end apart: 13 -> 0, of which waited for: 11 -> 0; matrix products, arithmetic and copies ran while one was open for 13% -> 0% of each run, Pallas kernels for 0% -> 0%
where the time goes in v1:
time: 236 us; the launch traced here: 235 us
  Pallas kernels  190 us (81%)
  local copies, waits for them, and re-layouts  42.3 us (18%)
  other arithmetic  2.49 us (1%)
    pallas_call x1, Pallas kernels, reduce_grads(): pl.pallas_call(functools.partial(rs_kernel, count, levels, rows, cols, la...  102 us
    pallas_call x1, Pallas kernels, both_passes(): pl.pallas_call(functools.partial(main_kernel, sizes), out_shape=(jax.Shap...  87.9 us
    pallas_call x2, local copies, waits for them, and re-layouts, both_passes(): pl.pallas_call(functools.partial(main_kernel, sizes), out_shape=(jax.Shap...  10.7 us
    reshape x1, local copies, waits for them, and re-layouts, reduce_grads(): dy = dy.reshape(deep, 27, cols).transpose(1, 0, 2)  10.2 us

profile of v1, /device:TPU:0, one launch (start us, length us, event | category | flops | bytes accessed | tf_op | source)
XLA Modules:
  0.0 235.3 jit_solution(11971141720230557451)
XLA Ops:
  0.7 0.1 pad.26.clone
  0.7 0.8 fusion.13
  1.6 1.3 copy.51
  2.9 0.8 fusion.12
  3.7 0.1 squeeze.27
  3.8 0.1 squeeze.29
  4.0 0.1 squeeze.28
  4.1 0.2 fusion.6
  4.2 0.2 copy.38
  4.5 0.9 copy.39.spread
  5.4 0.9 fusion.9.onehot
  6.3 87.9 %shard_map.195 = (bf16[512,768]{1,0:T(8,128)(2,1)}, f32[512,768]{1,0:T(8,128)}, bf16[5376,512]{1,0:T(8,128)(2,1)}, bf16[512,6912]{1,0:T(8,128)(2,1)}, f32[12,32,...) custom-call(s32[2]{0:T(128)} %lengths.1, bf16[512,768]{1,0:T(8,128)(2,1)} %tokens.1, ...), custom_call_target="tpu_custom_call" | custom-call | tf_op jit(solution)/shard_map/pallas_call | solution.py:384
  94.3 0.5 broadcast.58
  94.8 1.4 reduce.3
  96.2 0.1 reshape.98
  96.2 0.8 reshape.96
  97.1 0.1 reshape.97
  97.2 1.2 reshape.94
  98.4 0.1 copy.42
  98.5 0.1 reshape_reshape.3
  98.7 0.1 copy.43
  98.8 0.1 reshape.95
  98.9 0.7 copy.49
  99.6 10.2 %copy.40 = bf16[512,6912]{0,1:T(8,128)(2,1)} copy(bf16[512,6912]{1,0:T(8,128)(2,1)} %get-tuple-element.22) | data formatting | bytes 14155776 | tf_op jit(solution)/shard_map/pallas_call | solution.py:384
  109.8 10.2 %copy.41 = bf16[512,27,256]{2,0,1:T(8,128)(2,1)} copy(bf16[512,27,256]{0,2,1:T(8,128)(2,1)} %bitcast.42) | data formatting | bytes 14155776 | tf_op jit(solution)/shard_map/reshape | solution.py:554
  120.0 101.8 %shard_map.196 = (f32[48,9216]{1,0:T(8,128)}, f32[24,128]{1,0:T(8,128)}) custom-call(bf16[7,768,512]{2,1,0:T(8,128)(2,1)} %bitcast.43, bf16[27,512,256]{2,1,0:T(8,128)(2,1)} %bitcast.41, f32[16,24,128]{2,1,0:T(8,128)} %bitcast.54), custom_call_target="tpu_custom_call" | custom-call | tf_op jit(solution)/shard_map/pallas_call | solution.py:567
  221.8 0.0 copy-start.1
  221.8 1.3 slice.70
  223.1 0.7 slice.65
  223.8 0.1 reshape.103
  223.9 0.6 slice.66
  224.5 0.6 slice.69
  225.0 1.4 reshape.106
  226.4 1.6 slice_bitcast_fusion.2
  228.0 0.0 copy-start
  228.0 1.9 slice_bitcast_fusion.1
  229.9 2.1 fusion.11
  232.1 0.3 reshape.100
  232.4 0.9 copy.45
  233.3 0.0 copy-done.1
  233.3 0.9 copy.54
  234.2 0.0 copy-done
  234.2 1.1 copy.55
  (6 shorter events, 0.1 us)
Async XLA Ops:
  221.8 11.5 %copy-start.1 = (bf16[512,768]{1,0:T(8,128)(2,1)S(1)}, bf16[512,768]{1,0:T(8,128)(2,1)}, u32[]{:S(2)}) copy-start(bf16[512,768]{1,0:T(8,128)(2,1)} %get-tuple-element.19) | copy-start | bytes 2359300
  228.0 6.2 %copy-start = (f32[512,768]{1,0:T(8,128)S(1)}, f32[512,768]{1,0:T(8,128)}, u32[]{:S(2)}) copy-start(f32[512,768]{1,0:T(8,128)} %get-tuple-element.20) | copy-start | bytes 4718596

commit v2 on v1

v2 whole, which is shorter than its diff:
```python
import functools

import jax
import jax.numpy as jnp
from jax import lax
from jax.experimental import pallas as pl
from jax.experimental.pallas import tpu as pltpu
from jax.sharding import PartitionSpec as P

MESH = pl.DeviceIdType.MESH
BUCKETS = 32
LANES = 128
epsilon = 1e-05
masked_score = -1000000000.0
low = jnp.bfloat16
high = jnp.float32


def dot_nn(left, right):
    return jnp.dot(left, right, preferred_element_type=high)


def dot_nt(left, right):
    return lax.dot_general(left, right, (((1,), (1,)), ((), ())), preferred_element_type=high)


def normal_terms(values):
    below = 0.5 + 0.5 * lax.erf(values * 0.7071067811865476)
    return below, values * (0.3989422804014327 * jnp.exp(-0.5 * values * values))


def norm_rows(values):
    centered = values - jnp.mean(values, axis=-1, keepdims=True)
    spread = jnp.mean(centered * centered, axis=-1, keepdims=True)
    scale = lax.rsqrt(spread + epsilon)
    return centered * scale, scale


def norm_back(upstream, gain, normal, scale):
    scaled = upstream * gain
    middle = jnp.mean(scaled, axis=-1, keepdims=True)
    along = jnp.mean(scaled * normal, axis=-1, keepdims=True)
    return scale * (scaled - middle - normal * along)


def column_sum(values):
    return jnp.sum(values.astype(high), axis=0, keepdims=True)


def main_kernel(
    sizes, exchange,
    lengths, tokens, cotangent, buckets, layout, gains, offsets, bias,
    in_hbm, out_hbm, up_hbm, down_hbm,
    result, input_grads, plain_hbm, pair_hbm, full_hbm, right_hbm, cross_hbm, vectors, bias_grad, near_branch,
    w_in, w_out, w_up, w_down, arrive, arrive_grad, sent_grad,
    qkv, chance, context, normal_one, scale_one, normed, normed_low, slope, hidden,
    normal_two, scale_two, picked, work, square, square_low, cross, d_proj, d_att, d_before, d_branch,
    turned, turned_grad, back, d_context, d_first, onehot, spread, near_hidden, spun,
    load_sem, page_sem, spun_sem, right_sem, send_sem, recv_sem, near_send, near_recv,
):
    rows, width, heads, ff, pages = sizes
    size = width // heads
    pairs = heads // 2
    section = lax.axis_index("section")
    first = section == 0
    block = 64
    chunk = 512
    me = lax.axis_index("wide")
    side_bit = (me // 2) % 2
    near = me + 2 - 4 * side_bit
    slim = width // 2

    def near_copies(page):
        found = []
        for slot in range(ff // width):
            at = pl.multiple_of(slot * width + (1 - side_bit) * slim, LANES)
            found.append((hidden.at[page, :, pl.ds(at, slim)], near_hidden.at[page, :, pl.ds(slot * slim, slim)]))
        found.append((d_branch.at[page], near_branch.at[page_rows(page)]))
        return [
            pltpu.make_async_remote_copy(
                src_ref=src, dst_ref=dst, send_sem=near_send.at[page, slot], recv_sem=near_recv.at[page, slot],
                device_id={"wide": near}, device_id_type=MESH)
            for slot, (src, dst) in enumerate(found)
        ]

    def peer_copy(src, dst, slot):
        return pltpu.make_async_remote_copy(
            src_ref=src, dst_ref=dst, send_sem=send_sem.at[slot], recv_sem=recv_sem.at[slot],
            device_id={"section": 1 - section}, device_id_type=MESH)

    def page_rows(page):
        return pl.ds(pl.multiple_of(page * rows, rows), rows)

    loads = [pltpu.make_async_copy(src, dst, load_sem.at[at]) for at, (src, dst) in enumerate(
        ((in_hbm, w_in), (out_hbm, w_out), (up_hbm, w_up), (down_hbm, w_down)))]

    def own_copy(page):
        return pltpu.make_async_copy(tokens.at[page_rows(page)], arrive.at[page], page_sem.at[page])

    def own_grad_copy(page):
        return pltpu.make_async_copy(cotangent.at[page_rows(page)], arrive_grad.at[page], page_sem.at[page])

    @pl.when(first)
    def _():
        for page in range(pages):
            own_copy(page).start()

    for load in loads:
        load.start()

    @pl.when(section == 1)
    def _():
        for page in range(pages):
            own_grad_copy(page).start()

    barrier = pltpu.get_barrier_semaphore()
    pl.semaphore_signal(barrier, inc=1, device_id={"section": 1 - section}, device_id_type=MESH)
    if exchange:
        pl.semaphore_signal(barrier, inc=1, device_id={"wide": near}, device_id_type=MESH)
    pl.semaphore_wait(barrier, 2 if exchange else 1)

    onehot[...] = marks_of(buckets).T
    spread_tables(layout, spread)
    vectors[...] = jnp.zeros_like(vectors)
    bias_grad[...] = jnp.zeros_like(bias_grad)

    share = width // 16
    pieces = ff // width
    both = pages * rows

    def plain_copy(block):
        return pltpu.make_async_copy(
            spun.at[block % 2], plain_hbm.at[pl.ds(block * width, width)], spun_sem.at[block % 2, 0])

    def turn_plain():
        for block, source in enumerate((arrive, context, normed_low)):
            if block > 1:
                plain_copy(block - 2).wait()
            for page in range(pages):
                spun[block % 2, :, page * rows : (page + 1) * rows] = source[page].T
            plain_copy(block).start()
        for block in (1, 2):
            plain_copy(block).wait()

    def slab_copies(block, slot, pair, far):
        found = []
        for core in range(2):
            for piece in range(pieces):
                source = spun.at[slot, pl.ds((core * pieces + piece) * share, share)]
                row = pl.multiple_of((2 * block + core) * share, share)
                if pair:
                    target = pair_hbm.at[piece, pl.ds(row, share), pl.ds(far * both, both)]
                else:
                    target = full_hbm.at[piece, pl.ds(row, share)]
                found.append(pltpu.make_async_copy(source, target, spun_sem.at[slot, core * pieces + piece]))
        return found

    def turn_slabs(count, pair, far):
        def one(block, carry):
            slot = block % 2

            @pl.when(block > 1)
            def _():
                for copy in slab_copies(block - 2, slot, pair, far):
                    copy.wait()

            for page in range(pages):
                if far:
                    slab = near_hidden[page, :, pl.ds(pl.multiple_of(block * slim, LANES), slim)]
                elif pair:
                    slab = hidden[page, :, pl.ds(pl.multiple_of(block * width + side_bit * slim, LANES), slim)]
                else:
                    slab = hidden[page, :, pl.ds(pl.multiple_of(block * slim, LANES), slim)]
                spun[slot, 0:slim, page * rows : (page + 1) * rows] = slab.T
            for copy in slab_copies(block, slot, pair, far):
                copy.start()
            return carry

        lax.fori_loop(0, count, one, 0)
        for block in (count - 2, count - 1):
            for copy in slab_copies(block, block % 2, pair, far):
                copy.wait()

    def right_copies(page):
        found, at = [], 0
        for slot, piece in enumerate((d_proj, d_att, d_before, d_branch.at[page])):
            cols = piece.shape[-1]
            found.append(pltpu.make_async_copy(
                piece, right_hbm.at[page_rows(page), pl.ds(at, cols)], right_sem.at[page if slot == 3 else pages + slot]))
            at += cols
        found.append(pltpu.make_async_copy(cross, cross_hbm.at[page_rows(page)], right_sem.at[pages + 4]))
        return found

    lane = lax.broadcasted_iota(jnp.int32, (rows, LANES), 1)
    side = lane < size

    def result_copy(page):
        return peer_copy(result.at[page_rows(page)], arrive.at[page], page)

    def grad_copy(page):
        return peer_copy(sent_grad.at[page], arrive_grad.at[page], pages + page)

    def forward(page, carry):
        @pl.when(first)
        def _():
            own_copy(page).wait()

        @pl.when(section == 1)
        def _():
            result_copy(page).wait_recv()

        @pl.when(page == 0)
        def _():
            loads[0].wait()

        layer_in = arrive[page]
        for part in range(3):
            cols = slice(part * width, (part + 1) * width)
            found = dot_nn(layer_in, w_in[:, cols])
            if part != 1:
                found = found + offsets[part // 2]
            qkv[page, :, cols] = found.astype(low)
        mark = onehot[page_rows(page), :]
        for head in range(heads):
            picked[:, head * LANES : (head + 1) * LANES] = dot_nn(mark, spread[head]).astype(low)
        live = lax.broadcasted_iota(jnp.int32, (1, rows), 1) < lengths[page]
        zero = jnp.zeros((rows, LANES), low)
        for pair in range(pairs):
            cols = slice(pair * LANES, (pair + 1) * LANES)
            query = qkv[page, :, cols] * jnp.asarray(size**-0.5, low)
            keyed = jnp.concatenate([qkv[page, :, width + pair * LANES : width + (pair + 1) * LANES], mark], axis=1)
            valued = qkv[page, :, 2 * width + pair * LANES : 2 * width + (pair + 1) * LANES]
            found = []
            for half in range(2):
                head = 2 * pair + half
                mine = jnp.where(side if half == 0 else ~side, query, zero)
                full = jnp.concatenate([mine, picked[:, head * LANES : (head + 1) * LANES]], axis=1)
                square[half] = dot_nt(full, keyed)
            for half in range(2):
                head = 2 * pair + half
                for at in range(0, rows, block):
                    scores = jnp.where(live, square[half, at : at + block], masked_score)
                    raised = jnp.exp(scores - jnp.max(scores, axis=-1, keepdims=True))
                    share = raised * (1.0 / jnp.sum(raised, axis=-1, keepdims=True))
                    chance[page, head, at : at + block] = share
                    square_low[half, at : at + block] = share.astype(low)
            for half in range(2):
                found.append(dot_nn(square_low[half], valued))
            context[page, :, cols] = jnp.where(side, found[0], found[1]).astype(low)

        @pl.when(page == 0)
        def _():
            loads[1].wait()

        work[...] = dot_nn(context[page], w_out[...])

        for at in range(0, rows, block):
            here = slice(at, at + block)
            summed = arrive[page, here].astype(high) + (work[here] + offsets[2])
            normal, scale = norm_rows(summed)
            normal_one[page, here] = normal
            scale_one[page, here] = scale
            shifted = normal * gains[0:1] + offsets[3]
            normed[here] = shifted
            normed_low[page, here] = shifted.astype(low)

        @pl.when(page == 0)
        def _():
            loads[2].wait()
            loads[3].wait()

        for at in range(0, ff, chunk):
            cols = slice(at, at + chunk)
            before = dot_nn(normed_low[page], w_up[:, cols]) + bias[:, cols]
            below, density = normal_terms(before)
            hidden[page, :, cols] = (before * below).astype(low)
            slope[page, :, cols] = (below + density).astype(slope.dtype)
        if exchange:
            @pl.when(first)
            def _():
                for copy in near_copies(page)[:-1]:
                    copy.start()

        work[...] = dot_nn(hidden[page], w_down[...])
        for at in range(0, rows, block):
            here = slice(at, at + block)
            normal, scale = norm_rows(normed[here] + (work[here] + offsets[4]))
            normal_two[page, here] = normal
            scale_two[page, here] = scale
            result[pl.ds(pl.multiple_of(page * rows + at, block), block), :] = (
                normal * gains[1:2] + offsets[5]).astype(low)

        @pl.when(first)
        def _():
            result_copy(page).start()

        return carry

    lax.fori_loop(0, pages, forward, 0)

    @pl.when(first)
    def _():
        turn_plain()
        if exchange:
            turn_slabs(ff // width, True, 0)
            for page in range(pages):
                for copy in near_copies(page)[:-1]:
                    copy.wait()
            turn_slabs(ff // width, True, 1)
        else:
            turn_slabs(2 * ff // width, False, 0)

    def backward(page, carry):
        @pl.when(first)
        def _():
            grad_copy(page).wait_recv()

        @pl.when(section == 1)
        def _():
            own_grad_copy(page).wait()

        sums = [jnp.zeros((1, width), high) for _ in range(8)]
        for at in range(0, rows, block):
            here = slice(at, at + block)
            upstream = arrive_grad[page, here].astype(high)
            normal = normal_two[page, here]
            sums[1] += column_sum(upstream * normal)
            sums[7] += column_sum(upstream)
            d_second = norm_back(upstream, gains[1:2], normal, scale_two[page, here])
            d_first[here] = d_second
            branch = d_second.astype(low)
            sums[6] += column_sum(branch)
            d_branch[page, here] = branch
        right_copies(page)[3].start()
        if exchange:
            @pl.when(first)
            def _():
                near_copies(page)[-1].start()


        @pl.when(page > 0)
        def _():
            right_copies(page - 1)[2].wait()

        for at in range(0, ff, chunk):
            cols = slice(at, at + chunk)
            d_hidden = dot_nt(d_branch[page], w_down[cols, :])
            d_chunk = (d_hidden * slope[page, :, cols].astype(high)).astype(low)
            d_before[:, cols] = d_chunk
            bias_grad[:, cols] += column_sum(d_chunk)
        right_copies(page)[2].start()
        work[...] = dot_nt(d_before[...], w_up[...])

        @pl.when(page > 0)
        def _():
            right_copies(page - 1)[1].wait()

        for at in range(0, rows, block):
            here = slice(at, at + block)
            d_normed = d_first[here] + work[here]
            normal = normal_one[page, here]
            sums[0] += column_sum(d_normed * normal)
            sums[5] += column_sum(d_normed)
            found = norm_back(d_normed, gains[0:1], normal, scale_one[page, here])
            d_first[here] = found
            attended = found.astype(low)
            sums[4] += column_sum(attended)
            d_att[here] = attended
        right_copies(page)[1].start()
        d_context[...] = dot_nt(d_att[...], w_out[...]).astype(low)
        turned[...] = qkv[page, :, 0:width].T
        turned_grad[...] = d_context[...].T
        mark = onehot[page_rows(page), :]
        zero = jnp.zeros((rows, LANES), low)
        scaling = size**-0.5

        @pl.when(page > 0)
        def _():
            right_copies(page - 1)[0].wait()

        @pl.when(page > 0)
        def _():
            right_copies(page - 1)[4].wait()

        for pair in range(pairs):
            cols = slice(pair * LANES, (pair + 1) * LANES)
            keyed = jnp.concatenate([qkv[page, :, width + pair * LANES : width + (pair + 1) * LANES], mark], axis=1)
            valued = qkv[page, :, 2 * width + pair * LANES : 2 * width + (pair + 1) * LANES]
            given = d_context[:, cols]
            for half in range(2):
                mine = jnp.where(side if half == 0 else ~side, given, zero)
                square[half] = dot_nt(mine, valued)
            found = []
            for half in range(2):
                head = 2 * pair + half
                for at in range(0, rows, block):
                    share = chance[page, head, at : at + block]
                    both = share * square[half, at : at + block]
                    d_scores = both - share * jnp.sum(both, axis=-1, keepdims=True)
                    square_low[half, at : at + block] = d_scores.astype(low)
            for half in range(2):
                head = 2 * pair + half
                slim = slice(head * size, (head + 1) * size)
                both = dot_nn(square_low[half], keyed)
                found.append(both[:, :LANES])
                rest = both[:, LANES:]
                upper = rest.astype(low)
                lower = (rest - upper.astype(high)).astype(low)
                cross[:, 2 * head * LANES : (2 * head + 1) * LANES] = upper
                cross[:, (2 * head + 1) * LANES : (2 * head + 2) * LANES] = lower
                back[slim, :] = dot_nn(turned[slim, :], square_low[half]) * scaling
                back[slice(width + head * size, width + (head + 1) * size), :] = dot_nn(
                    turned_grad[slim, :], chance[page, head].astype(low))
            d_proj[:, cols] = (jnp.where(side, found[0], found[1]) * scaling).astype(low)
        d_proj[:, width:] = back[...].astype(low).T
        sums[2] += column_sum(d_proj[:, 0:width])
        sums[3] += column_sum(d_proj[:, 2 * width :])
        for row, value in enumerate(sums):
            vectors[row : row + 1, :] += value
        right_copies(page)[0].start()
        right_copies(page)[4].start()
        work[...] = dot_nt(d_proj[...], w_in[...])
        for at in range(0, rows, block):
            here = slice(at, at + block)
            d_in = d_first[here] + work[here]
            narrow = d_in.astype(low)
            sent_grad[page, here] = narrow
            input_grads[pl.ds(pl.multiple_of(page * rows + at, block), block), :] = jnp.where(
                first, d_in, narrow.astype(high))

        @pl.when(section == 1)
        def _():
            grad_copy(page).start()

        return carry

    lax.fori_loop(0, pages, backward, 0)

    @pl.when(section == 1)
    def _():
        turn_plain()
        turn_slabs(2 * ff // width, False, 0)

    for page in range(pages):
        right_copies(page)[3].wait()
        if exchange:
            @pl.when(first)
            def _():
                near_copies(page)[-1].wait()

    for slot in (0, 1, 2, 4):
        right_copies(pages - 1)[slot].wait()
    for page in range(pages):
        @pl.when(first)
        def _():
            result_copy(page).wait_send()

        @pl.when(section == 1)
        def _():
            grad_copy(page).wait_send()


def both_passes(tokens, cotangent, lengths, buckets, layout, params, exchange):
    in_proj, out_proj, up_proj, down_proj, gains, offsets, bias, heads = params
    pages = lengths.shape[0]
    rows = tokens.shape[0] // pages
    width, ff = up_proj.shape
    sizes = (rows, width, heads, ff, pages)
    VM = pltpu.VMEM
    here, there = pl.BlockSpec(memory_space=pltpu.VMEM), pl.BlockSpec(memory_space=pl.ANY)
    scratch = [
        VM(in_proj.shape, low), VM(out_proj.shape, low), VM(up_proj.shape, low), VM(down_proj.shape, low),
        VM((pages, rows, width), low), VM((pages, rows, width), low), VM((pages, rows, width), low),
        VM((pages, rows, 3 * width), low),
        VM((pages, heads, rows, rows), high),
        VM((pages, rows, width), low),
        VM((pages, rows, width), high), VM((pages, rows, 1), high),
        VM((rows, width), high), VM((pages, rows, width), low),
        VM((pages, rows, ff), high),
        VM((pages, rows, ff), low),
        VM((pages, rows, width), high), VM((pages, rows, 1), high),
        VM((rows, heads * LANES), low),
        VM((rows, width), high),
        VM((2, rows, rows), high), VM((2, rows, rows), low),
        VM((rows, 2 * heads * LANES), low),
        VM((rows, 3 * width), low), VM((rows, width), low), VM((rows, ff), low), VM((pages, rows, width), low),
        VM((width, rows), low), VM((width, rows), low), VM((2 * width, rows), high),
        VM((rows, width), low), VM((rows, width), high),
        VM((pages * rows, LANES), low), VM((heads, LANES, LANES), low),
        VM((pages, rows, ff // 2), low), VM((2, width, pages * rows), low),
        pltpu.SemaphoreType.DMA((4,)), pltpu.SemaphoreType.DMA((pages,)), pltpu.SemaphoreType.DMA((2, 2 * ff // width)),
        pltpu.SemaphoreType.DMA((pages + 5,)), pltpu.SemaphoreType.DMA((2 * pages,)), pltpu.SemaphoreType.DMA((2 * pages,)),
        pltpu.SemaphoreType.DMA((pages, ff // width + 1)), pltpu.SemaphoreType.DMA((pages, ff // width + 1)),
    ]
    return pl.pallas_call(
        functools.partial(main_kernel, sizes, exchange),
        out_shape=(
            jax.ShapeDtypeStruct(tokens.shape, low),
            jax.ShapeDtypeStruct(tokens.shape, high),
            jax.ShapeDtypeStruct((3 * width, pages * rows), low),
            jax.ShapeDtypeStruct((ff // width, width // 2, 2 * pages * rows), low),
            jax.ShapeDtypeStruct((ff // width, width, pages * rows), low),
            jax.ShapeDtypeStruct((pages * rows, 5 * width + ff), low),
            jax.ShapeDtypeStruct((pages * rows, 2 * heads * LANES), low),
            jax.ShapeDtypeStruct((8, width), high),
            jax.ShapeDtypeStruct((1, ff), high),
            jax.ShapeDtypeStruct((pages * rows, width), low),
        ),
        in_specs=[pl.BlockSpec(memory_space=pltpu.SMEM), there, there, here, here, here, here, here] + [there] * 4,
        out_specs=(here, here, there, there, there, there, there, here, here, there),
        scratch_shapes=scratch,
        compiler_params=pltpu.CompilerParams(
            collective_id=0, has_side_effects=True, vmem_limit_bytes=63 * 2**20),
    )(lengths, tokens, cotangent, buckets, layout, gains, offsets, bias, in_proj, out_proj, up_proj, down_proj)


def marks_of(buckets):
    tokens = buckets.shape[1]
    level = lax.broadcasted_iota(jnp.int32, (BUCKETS, tokens), 0)
    rows = [jnp.where(buckets[axis : axis + 1, :] == level, 1.0, 0.0) for axis in range(3)]
    return jnp.concatenate(rows + [jnp.zeros((BUCKETS, tokens), high)], axis=0).astype(low)


def spread_tables(layout, spread):
    cells = BUCKETS * BUCKETS
    row = lax.broadcasted_iota(jnp.int32, (BUCKETS, cells), 0)
    own = lax.broadcasted_iota(jnp.int32, (BUCKETS, cells), 1) // BUCKETS == row
    cell = lax.broadcasted_iota(jnp.int32, (cells, LANES), 0) % BUCKETS
    place = lax.broadcasted_iota(jnp.int32, (cells, LANES), 1)
    heads = layout.shape[1]
    for axis in range(3):
        cellwise = layout[axis].astype(high)
        target = jnp.where(cell + axis * BUCKETS == place, 1.0, 0.0).astype(low)
        for head in range(heads):
            grid = jnp.where(own, cellwise[head : head + 1], 0.0).astype(low)
            spread[head, axis * BUCKETS : (axis + 1) * BUCKETS] = dot_nn(grid, target).astype(low)
    spread[:, 3 * BUCKETS :] = jnp.zeros((heads, LANES - 3 * BUCKETS, LANES), low)


def cross_tables(turned, cross):
    found = dot_nn(turned, cross)
    found = found[:, :LANES] + found[:, LANES:]
    place = lax.broadcasted_iota(jnp.int32, (BUCKETS, LANES), 1)
    return jnp.where(
        place < BUCKETS, found[:BUCKETS],
        jnp.where(place < 2 * BUCKETS, found[BUCKETS : 2 * BUCKETS], found[2 * BUCKETS : 3 * BUCKETS]))


LAGS = ((0, 2, 7, 12, 17), (0, 1, 3, 8, 13))


def down_turn(turn):
    return jnp.logical_or(turn == 35, jnp.logical_and(turn < 33, turn % 3 == 0))


def down_of(turn):
    return jnp.where(turn == 35, 11, turn // 3)


def place_of(turn):
    other = jnp.where(turn < 33, 2 * (turn // 3) + turn % 3 - 1, turn - 11)
    other = jnp.where(other < 12, other + 12, jnp.where(other < 15, other - 3, other - 15))
    return jnp.where(down_turn(turn), 24 + down_of(turn), other)


def left_of(at):
    return jnp.where(at < 9, 0, jnp.where(at < 12, 1, 2))


def rs_kernel(
    count, levels, rows, cols, lags,
    plain_hbm, pair_hbm, full_hbm, right_hbm, cross_hbm, near_branch, buckets, vectors, bias_grad,
    out_in, out_out, out_up, out_down, out_tables, out_gains, out_offsets, out_bias,
    left, left_pair, left_full, right, right_down, cross, tables, dw, k1, k2, k3, s0, s1, s2, s3, r0, r1, r2, r3, ssem, rsem, left_sem, right_sem, left_down_sem, right_down_sem, cross_sem,
    ks, ks0, ks1, ks2, ss0, ss1, ss2, ss3, sr0, sr1, sr2, sr3, sssem, srsem,
):
    me = lax.axis_index("wide")
    keeps, sends, recvs = (dw, k1, k2, k3), (s0, s1, s2, s3), (r0, r1, r2, r3)
    skeeps, ssends, srecvs = (ks, ks0, ks1, ks2), (ss0, ss1, ss2, ss3), (sr0, sr1, sr2, sr3)
    bits = [(me // 2**level) % 2 for level in range(levels)]
    partners = [me + 2**level * (1 - 2 * bits[level]) for level in range(levels)]
    width = rows * 2**levels

    section = lax.axis_index("section")
    first = section == 0
    depth = right.shape[1]

    def left_load(block):
        return pltpu.make_async_copy(
            plain_hbm.at[pl.ds(pl.multiple_of(block * width, width), width)], left.at[block], left_sem.at[block])

    def right_load(block):
        return pltpu.make_async_copy(
            right_hbm.at[:, pl.ds(pl.multiple_of(block * cols, cols), cols)], right.at[block], right_sem.at[block])

    def pair_load(piece):
        return pltpu.make_async_copy(pair_hbm.at[piece], left_pair.at[piece], left_down_sem.at[piece])

    def full_load(piece):
        return pltpu.make_async_copy(full_hbm.at[piece], left_full.at[piece], left_down_sem.at[piece])

    def right_down_load(col):
        here = pl.ds(pl.multiple_of((right.shape[0] + col) * cols, cols), cols)
        return pltpu.make_async_copy(right_hbm.at[:, here], right_down.at[col, pl.ds(0, depth)], right_down_sem.at[0, col])

    def near_load(col):
        there = pl.ds(pl.multiple_of(col * cols, cols), cols)
        return pltpu.make_async_copy(near_branch.at[:, there], right_down.at[col, pl.ds(depth, depth)], right_down_sem.at[1, col])

    cross_load = pltpu.make_async_copy(cross_hbm, cross, cross_sem)
    barrier = pltpu.get_barrier_semaphore()
    for partner in partners:
        pl.semaphore_signal(barrier, inc=1, device_id={"wide": partner}, device_id_type=MESH)

    @pl.when(first)
    def _():
        pair_load(0).start()
        near_load(0).start()

    @pl.when(section == 1)
    def _():
        full_load(0).start()

    right_down_load(0).start()
    left_load(2).start()
    for block in range(12, 16):
        right_load(block).start()
    for col in (1, 2):
        right_down_load(col).start()

    @pl.when(first)
    def _():
        for col in (1, 2):
            near_load(col).start()
        for piece in (1, 2, 3):
            pair_load(piece).start()

    @pl.when(section == 1)
    def _():
        for piece in (1, 2, 3):
            full_load(piece).start()

    for block in range(16, 24):
        right_load(block).start()
    cross_load.start()
    for block in (1, 0):
        left_load(block).start()
    for block in range(0, 12):
        right_load(block).start()
    pl.semaphore_wait(barrier, levels)

    def copy(step, at, partner):
        return pltpu.make_async_remote_copy(
            src_ref=sends[step].at[at], dst_ref=recvs[step].at[at],
            send_sem=ssem.at[step, at], recv_sem=rsem.at[step, at],
            device_id={"wide": partners[partner]}, device_id_type=MESH)

    def small_copy(step):
        return pltpu.make_async_remote_copy(
            src_ref=ssends[step], dst_ref=srecvs[step],
            send_sem=sssem.at[step], recv_sem=srsem.at[step],
            device_id={"wide": partners[step]}, device_id_type=MESH)

    def cross_head(head):
        here = pl.ds(pl.multiple_of(head * 2 * LANES, 2 * LANES), 2 * LANES)
        tables[head] = cross_tables(marks_of(buckets), cross[:, here])

    def paired(turn):
        return jnp.logical_and(first, down_turn(turn))

    def far_first(turn):
        return jnp.logical_and(section == 1, turn % 6 == 0)

    def start(turn):
        at = place_of(turn)
        slot = turn % dw.shape[0]
        down = down_of(turn)
        piece, col = down // 3, down % 3

        def take(value):
            dw[slot] = value.reshape(dw.shape[1:])
            for j in range(2 ** (levels - 1)):
                s0[turn, j] = dw[slot, 2 * j + 1 - bits[0]].astype(low)
            copy(0, turn, 0).start()

        @pl.when(jnp.logical_and(down_turn(turn), down < 3))
        def _():
            right_down_load(down).wait()

        @pl.when(paired(turn))
        def _():
            @pl.when(down < 3)
            def _():
                near_load(down).wait()

            @pl.when(col == 0)
            def _():
                pair_load(piece).wait()

            found = dot_nn(left_pair[piece], right_down[col])
            dw[slot, 0 : 2 ** (levels - 1)] = found.reshape((2 ** (levels - 1),) + dw.shape[2:])

        @pl.when(jnp.logical_and(section == 1, down_turn(turn)))
        def _():
            @pl.when(col == 0)
            def _():
                full_load(piece).wait()

            take(dot_nn(left_full[piece], right_down[col, 0:depth]))

        @pl.when(jnp.logical_not(down_turn(turn)))
        def _():
            right_load(at).wait()

            @pl.when(jnp.logical_or(at == 12, jnp.logical_or(at == 9, at == 0)))
            def _():
                left_load(left_of(at)).wait()

            take(dot_nn(left[left_of(at)], right[at]))

    def pass_on(step, at, partner, place, total):
        half = 2 ** (levels - 1 - step)
        new = at % keeps[step].shape[0]
        bit = bits[partner]

        def pick(j, value):
            return (j >> place << (place + 1)) + (j & (2**place - 1)) + value * 2**place

        for j in range(half):
            sends[step][at, j] = total(pick(j, 1 - bit)).astype(low)
        copy(step, at, partner).start()
        for j in range(half):
            keeps[step][new, j] = total(pick(j, bit))

    def second(at, kind):
        old = at % dw.shape[0]
        if kind == "paired":
            pass_on(1, at, 0, 0, lambda pick: dw[old, pick])
            return
        copy(0, at, 0).wait_recv()
        partner, place = (2, 1) if kind == "far" else (1, 0)
        pass_on(1, at, partner, place, lambda pick: dw[old, 2 * pick + bits[0]] + r0[at, pick].astype(high))

    def later(step, at, kind):
        copy(step - 1, at, 0).wait_recv()
        old = at % keeps[step - 1].shape[0]
        partner, place = ((3, 1) if step == 2 else (1, 0)) if kind == "far" else (step, 0)
        pass_on(step, at, partner, place, lambda pick: keeps[step - 1][old, pick] + recvs[step - 1][at, pick].astype(high))

    def finish(turn):
        copy(levels - 1, turn, levels - 1).wait_recv()
        old = turn % keeps[levels - 1].shape[0]
        value = keeps[levels - 1][old, 0] + recvs[levels - 1][turn, 0].astype(high)
        at = place_of(turn)

        def columns(first):
            return pl.ds(pl.multiple_of((at - first) * cols, cols), cols)

        @pl.when(at < 9)
        def _():
            out_in[0, :, columns(0)] = value

        @pl.when(jnp.logical_and(at >= 9, at < 12))
        def _():
            out_out[0, :, columns(9)] = value

        @pl.when(jnp.logical_and(at >= 12, at < 24))
        def _():
            out_up[0, :, columns(12)] = value

        @pl.when(at >= 24)
        def _():
            part, col = (at - 24) // 3, at % 3
            out_down[0, pl.ds(pl.multiple_of(part * rows, rows), rows), pl.ds(pl.multiple_of(col * cols, cols), cols)] = value

    def small_fill():
        heads = tables.shape[0]
        for part in range(2**levels):
            for head in range(heads):
                ks[part, 2 * head : 2 * head + 2] = tables[head, 2 * part : 2 * part + 2]
            ks[part, 2 * heads : 2 * heads + 8, 0:rows] = vectors[:, part * rows : (part + 1) * rows]
            for piece in range(4):
                at = (4 * part + piece) * rows
                ks[part, 2 * heads + piece : 2 * heads + piece + 1, rows : 2 * rows] = bias_grad[:, at : at + rows]

    def small_stage(step):
        if step:
            small_copy(step - 1).wait_recv()
        if step == levels:
            heads = tables.shape[0]
            ks[0] = skeeps[levels - 1][0] + srecvs[levels - 1][0]
            for axis in range(3):
                for i in range(2):
                    got = ks[0, pl.ds(i, heads, 2), :]
                    out_tables[axis, :, 0, i * BUCKETS : (i + 1) * BUCKETS] = got[:, axis * BUCKETS : (axis + 1) * BUCKETS]
            out_gains[0] = ks[0, 2 * heads : 2 * heads + 2, 0:rows]
            out_offsets[:, 0] = ks[0, 2 * heads + 2 : 2 * heads + 8, 0:rows]
            for piece in range(4):
                out_bias[:, piece * rows : (piece + 1) * rows] = ks[0, 2 * heads + piece : 2 * heads + piece + 1, rows : 2 * rows]
            return
        half = 2 ** (levels - 1 - step)

        def total(pick):
            if step == 0:
                return ks[pick]
            return skeeps[step - 1][2 * pick + bits[0] if step == 1 else pick] + srecvs[step - 1][pick]

        for j in range(half):
            ssends[step][j] = total(2 * j + 1 - bits[step])
        small_copy(step).start()
        if step:
            for j in range(half):
                skeeps[step][j] = total(2 * j + bits[step])

    def step_at(moment, carry):
        @pl.when(moment == 5)
        def _():
            cross_load.wait()

        @pl.when(jnp.logical_and(moment >= 5, moment < 5 + tables.shape[0]))
        def _():
            cross_head(moment - 5)

        def due(at):
            return jnp.logical_and(at >= 0, at < count)

        @pl.when(due(moment))
        def _():
            start(moment)

        for step in range(1, levels + 1):
            near_at, pair_at = moment - lags[0][step], moment - lags[1][step]
            plain_due = jnp.logical_and(due(near_at), jnp.logical_not(paired(near_at)))
            pair_due = jnp.logical_and(due(pair_at), paired(pair_at))
            if step == 1:
                @pl.when(pair_due)
                def _():
                    second(pair_at, "paired")
            elif step < levels:
                @pl.when(pair_due)
                def _():
                    later(step, pair_at, "paired")
            else:
                @pl.when(pair_due)
                def _():
                    finish(pair_at)

                @pl.when(plain_due)
                def _():
                    finish(near_at)
                continue
            for kind in ("plain", "far"):
                chosen = far_first(near_at) if kind == "far" else jnp.logical_not(far_first(near_at))

                @pl.when(jnp.logical_and(plain_due, chosen))
                def _():
                    second(near_at, kind) if step == 1 else later(step, near_at, kind)
        return carry

    ks[...] = jnp.zeros_like(ks)
    lax.fori_loop(0, 19, step_at, 0)
    small_fill()
    small_stage(0)
    lax.fori_loop(19, 22, step_at, 0)
    small_stage(1)
    lax.fori_loop(22, count, step_at, 0)
    small_stage(2)
    small_stage(3)
    small_stage(4)
    lax.fori_loop(count, count + lags[0][levels], step_at, 0)

    def drain(at, carry):
        @pl.when(jnp.logical_not(paired(at)))
        def _():
            copy(0, at, 0).wait_send()

        for step in range(1, levels):
            copy(step, at, step).wait_send()
        return carry

    lax.fori_loop(0, count, drain, 0)
    for step in range(levels):
        small_copy(step).wait_send()


def reduce_grads(plain, pair, full, right, cross, near_branch, buckets, vectors, bias_grad, count=36, levels=4, lags=LAGS):
    n = 2**levels
    depth, total = right.shape
    width = vectors.shape[1]
    cols, rows = 256, width // n
    heads = cross.shape[1] // (2 * LANES)
    ff = bias_grad.shape[1]
    others = total // cols - width // cols

    def ring(step):
        return max(lag[step + 1] for lag in lags) - min(lag[step] for lag in lags) + 1

    VM = pltpu.VMEM
    scratch = [VM((3, width, depth), low), VM(pair.shape, low), VM(full.shape, low)]
    scratch += [VM((others, depth, cols), low), VM((width // cols, 2 * depth, cols), low)]
    scratch += [VM(cross.shape, low), VM((heads, BUCKETS, LANES), high)]
    scratch += [VM((ring(0), n, rows, cols), high)]
    scratch += [VM((ring(step), n >> (step + 1), rows, cols), high) for step in (1, 2, 3)]
    scratch += [VM((count, n >> (step + 1), rows, cols), low) for step in range(4)] * 2
    scratch += [pltpu.SemaphoreType.DMA((levels, count))] * 2
    scratch += [pltpu.SemaphoreType.DMA((3,)), pltpu.SemaphoreType.DMA((others,))]
    scratch += [pltpu.SemaphoreType.DMA((ff // width,)), pltpu.SemaphoreType.DMA((2, width // cols)), pltpu.SemaphoreType.DMA]
    few = (2 * heads + 8, LANES)
    scratch += [VM((n,) + few, high)]
    scratch += [VM((n >> (step + 1),) + few, high) for step in (1, 2, 3)]
    scratch += [VM((n >> (step + 1),) + few, high) for step in range(4)] * 2
    scratch += [pltpu.SemaphoreType.DMA((levels,))] * 2
    here, there = pl.BlockSpec(memory_space=pltpu.VMEM), pl.BlockSpec(memory_space=pl.ANY)
    shapes = (
        (1, rows, 3 * width), (1, rows, width), (1, rows, ff), (1, ff // n, width),
        (3, heads, 1, 2 * BUCKETS), (1, 2, rows), (6, 1, rows), (1, ff // n),
    )
    return pl.pallas_call(
        functools.partial(rs_kernel, count, levels, rows, cols, lags),
        out_shape=tuple(jax.ShapeDtypeStruct(shape, high) for shape in shapes),
        in_specs=[there] * 6 + [here] * 3,
        out_specs=(here,) * len(shapes),
        scratch_shapes=scratch,
        compiler_params=pltpu.CompilerParams(
            collective_id=1, has_side_effects=True, vmem_limit_bytes=63 * 2**20),
    )(plain, pair, full, right, cross, near_branch, buckets, vectors, bias_grad)


def settle_kernel(count, *refs):
    sources, targets, held, sem = refs[:count], refs[count : 2 * count], refs[2 * count : 3 * count], refs[3 * count]
    copies = [
        (pltpu.make_async_copy(sources[at], held[at], sem.at[0, at]), pltpu.make_async_copy(held[at], targets[at], sem.at[1, at]))
        for at in range(count)
    ]
    for fetch, _ in copies:
        fetch.start()
    for fetch, put in copies:
        fetch.wait()
        put.start()
    for _, put in copies:
        put.wait()


def settle(arrays):
    there = pl.BlockSpec(memory_space=pl.ANY)
    return pl.pallas_call(
        functools.partial(settle_kernel, len(arrays)),
        out_shape=tuple(jax.ShapeDtypeStruct(array.shape, array.dtype) for array in arrays),
        in_specs=[there] * len(arrays),
        out_specs=(there,) * len(arrays),
        scratch_shapes=[pltpu.VMEM(array.shape, array.dtype) for array in arrays] + [pltpu.SemaphoreType.DMA((2, len(arrays)))],
        compiler_params=pltpu.CompilerParams(vmem_limit_bytes=63 * 2**20),
    )(*arrays)


def local(tokens, cotangent, lengths, buckets, in_proj, out_proj, up_proj, down_proj, layout_tables, norm_gains, offsets, hidden_bias):
    heads = layout_tables.shape[2]
    width, ff = up_proj.shape[1:]
    shifts = jnp.transpose(offsets, (1, 0, 2))
    params = (in_proj[0], out_proj[0], up_proj[0], down_proj[0], norm_gains[0], shifts, hidden_bias, heads)
    wide_count = lax.axis_size("wide")
    result, input_grads, plain, pair, full, right, cross, vectors, bias_grad, near_branch = both_passes(
        tokens, cotangent, lengths, buckets, layout_tables[0], params, wide_count == 16)
    share = width // wide_count
    if wide_count == 16 and share % 16 == 0:
        found = reduce_grads(plain, pair, full, right, cross, near_branch, buckets, vectors, bias_grad)
        found = settle((result[None], input_grads[None]) + found)
        return found[:6] + (jnp.transpose(found[6], (2, 0, 1, 3)), found[7], jnp.transpose(found[8], (1, 0, 2)), found[9])
    else:

        def scattered(value, dim):
            return lax.psum_scatter(value[None], "wide", scatter_dimension=dim, tiled=True)

        def product(rows_from, cols_from, cols):
            return dot_nn(plain[rows_from : rows_from + width], right[:, cols_from : cols_from + cols])

        grad_in = scattered(product(0, 0, 3 * width), 1)
        grad_out = scattered(product(width, 3 * width, width), 1)
        grad_up = scattered(product(2 * width, 4 * width, ff), 1)
        grad_down = dot_nn(full.reshape(ff, -1), right[:, 4 * width + ff :])
        grad_down = grad_down.reshape(ff // width, 16, -1, width).transpose(1, 0, 2, 3).reshape(ff, width)
        grad_down = scattered(grad_down, 1)
        grad_hidden = scattered(bias_grad[0], 1)
        turned = marks_of(buckets)
        tables = jnp.stack([
            cross_tables(turned, cross[:, 2 * head * LANES : 2 * (head + 1) * LANES]) for head in range(heads)])
        tables = tables[:, :, : 3 * BUCKETS].reshape(heads, BUCKETS, 3, BUCKETS).transpose(2, 0, 1, 3)
        grad_tables = scattered(tables.reshape(3, heads, -1), 3)
        vectors = scattered(vectors, 2)
        grad_gains, grad_offsets = vectors[:, :2], vectors[:, 2:]
    return (
        result[None],
        input_grads[None],
        grad_in,
        grad_out,
        grad_up,
        grad_down,
        grad_tables,
        grad_gains,
        grad_offsets,
        grad_hidden,
    )


def solution(mesh):
    placed = (
        P("wide", None),
        P("wide", None),
        P("wide"),
        P(None, "wide"),
        P("section", None, None),
        P("section", None, None),
        P("section", None, None),
        P("section", None, None),
        P("section", None, None, None),
        P("section", None, None),
        P("section", None, None),
        P("section", None),
    )
    return jax.shard_map(
        local,
        mesh=mesh,
        in_specs=placed,
        out_specs=(
            P("section", "wide", None),
            P("section", "wide", None),
            P("section", "wide", None),
            P("section", "wide", None),
            P("section", "wide", None),
            P("section", "wide", None),
            P("section", None, None, "wide"),
            P("section", None, "wide"),
            P("section", None, "wide"),
            P("section", "wide"),
        ),
        check_vma=False,
    )
```

time: 236 us -> 168 us (0.71)
  local copies, waits for them, and re-layouts: 42.3 us -> 0 us
  Pallas kernels: 190 us -> 167 us
  other arithmetic: 2.49 us -> 0 us
    pallas_call x1, Pallas kernels: 102 us -> 80.4 us  [reduce_grads(): pl.pallas_call(functools.partial(rs_kernel, count, levels, rows, cols, la...]
    reshape x10 -> x0, local copies, waits for them, and re-layouts: 15.3 us -> none  [the longest x1 10.2 us: reduce_grads(): dy = dy.reshape(deep, 27, cols).transpose(1, 0, 2)]
    pallas_call x2 -> x0, local copies, waits for them, and re-layouts: 10.7 us -> none  [both_passes(): pl.pallas_call(functools.partial(main_kernel, sizes), out_shape=(jax.Shap...]
    slice x7 -> x0, local copies, waits for them, and re-layouts: 6.88 us -> none  [the longest x1 2.13 us: local(): grad_down = grads[:, 4 * width + ff:].reshape(share, deep, width)]
    unnamed x8 -> x0, local copies, waits for them, and re-layouts: 4.08 us -> none
    broadcast_in_dim x3 -> x0, local copies, waits for them, and re-layouts: 3.5 us -> none  [the longest x1 1.92 us: local(): grad_in = grads[None, :, :3 * width]]
    pallas_call x1 -> x2, Pallas kernels: 87.9 us -> 86.2 us  [the longest x1 82.6 us: both_passes(): pl.pallas_call(functools.partial(main_kernel, sizes, exchange), out_shape...]
where the time goes in v2:
time: 168 us; the launch traced here: 167 us
  Pallas kernels  167 us (99%)
    pallas_call x1, Pallas kernels, both_passes(): pl.pallas_call(functools.partial(main_kernel, sizes, exchange), out_shape...  82.6 us
    pallas_call x1, Pallas kernels, reduce_grads(): pl.pallas_call(functools.partial(rs_kernel, count, levels, rows, cols, la...  80.4 us
    pallas_call x1, Pallas kernels, settle(): pl.pallas_call(functools.partial(settle_kernel, len(arrays)), out_shape=t...  3.57 us

profile of v2, /device:TPU:0, one launch (start us, length us, event | category | flops | bytes accessed | tf_op | source)
XLA Modules:
  0.0 167.4 jit_solution(67836926781186509)
XLA Ops:
  0.6 82.6 %shard_map.195 = (bf16[512,768]{1,0:T(8,128)(2,1)}, f32[512,768]{1,0:T(8,128)}, bf16[2304,512]{1,0:T(8,128)(2,1)}, bf16[4,384,1024]{2,1,0:T(8,128)(2,1)}, bf16[4...) custom-call(s32[2]{0:T(128)} %lengths.1, ...), custom_call_target="tpu_custom_call" | custom-call | tf_op jit(solution)/shard_map/pallas_call | solution.py:495
  83.2 80.4 %shard_map.196 = (f32[1,48,2304]{2,1,0:T(8,128)}, f32[1,48,768]{2,1,0:T(8,128)}, f32[1,48,3072]{2,1,0:T(8,128)}, f32[1,192,768]{2,1,0:T(8,128)}, f32[3,12,1,64]{...) custom-call(bf16[2304,512]{1,0:T(8,128)(2,1)} %get-tuple-element.40.plain_hbm, ...), custom_call_target="tpu_custom_call" | custom-call | tf_op jit(solution)/shard_map/pallas_call | solution.py:918
  163.6 3.6 %shard_map.197 = (bf16[1,512,768]{2,1,0:T(8,128)(2,1)}, f32[1,512,768]{2,1,0:T(8,128)}, f32[1,48,2304]{2,1,0:T(8,128)}, f32[1,48,768]{2,1,0:T(8,128)}, f32[1,48,...) custom-call(bf16[1,512,768]{2,1,0:T(8,128)(2,1)} %bitcast.16, ...), custom_call_target="tpu_custom_call" | custom-call | tf_op jit(solution)/shard_map/pallas_call | solution.py:946

commit v3 on v2

--- a/solution.py
+++ b/solution.py
@@ -194,11 +194,14 @@
     lane = lax.broadcasted_iota(jnp.int32, (rows, LANES), 1)
     side = lane < size
 
-    def result_copy(page):
-        return peer_copy(result.at[page_rows(page)], arrive.at[page], page)
+    tall = rows // 2
+
+    def result_copy(page, part):
+        here = pl.ds(pl.multiple_of(page * rows + part * tall, tall), tall)
+        return peer_copy(result.at[here], arrive.at[page, pl.ds(part * tall, tall)], 2 * page + part)
 
     def grad_copy(page):
-        return peer_copy(sent_grad.at[page], arrive_grad.at[page], pages + page)
+        return peer_copy(sent_grad.at[page], arrive_grad.at[page], 2 * pages + page)
 
     def forward(page, carry):
         @pl.when(first)
@@ -207,7 +210,8 @@
 
         @pl.when(section == 1)
         def _():
-            result_copy(page).wait_recv()
+            for part in range(2):
+                result_copy(page, part).wait_recv()
 
         @pl.when(page == 0)
         def _():
@@ -225,28 +229,37 @@
             picked[:, head * LANES : (head + 1) * LANES] = dot_nn(mark, spread[head]).astype(low)
         live = lax.broadcasted_iota(jnp.int32, (1, rows), 1) < lengths[page]
         zero = jnp.zeros((rows, LANES), low)
-        for pair in range(pairs):
+
+        def scores_of(pair):
             cols = slice(pair * LANES, (pair + 1) * LANES)
             query = qkv[page, :, cols] * jnp.asarray(size**-0.5, low)
             keyed = jnp.concatenate([qkv[page, :, width + pair * LANES : width + (pair + 1) * LANES], mark], axis=1)
-            valued = qkv[page, :, 2 * width + pair * LANES : 2 * width + (pair + 1) * LANES]
-            found = []
+            parts = []
             for half in range(2):
                 head = 2 * pair + half
                 mine = jnp.where(side if half == 0 else ~side, query, zero)
-                full = jnp.concatenate([mine, picked[:, head * LANES : (head + 1) * LANES]], axis=1)
-                square[half] = dot_nt(full, keyed)
-            for half in range(2):
-                head = 2 * pair + half
-                for at in range(0, rows, block):
-                    scores = jnp.where(live, square[half, at : at + block], masked_score)
-                    raised = jnp.exp(scores - jnp.max(scores, axis=-1, keepdims=True))
-                    share = raised * (1.0 / jnp.sum(raised, axis=-1, keepdims=True))
-                    chance[page, head, at : at + block] = share
-                    square_low[half, at : at + block] = share.astype(low)
-            for half in range(2):
-                found.append(dot_nn(square_low[half], valued))
-            context[page, :, cols] = jnp.where(side, found[0], found[1]).astype(low)
+                parts.append(jnp.concatenate([mine, picked[:, head * LANES : (head + 1) * LANES]], axis=1))
+            square[pair % 2] = dot_nt(jnp.concatenate(parts, axis=0), keyed)
+
+        def attend(pair):
+            cols = slice(pair * LANES, (pair + 1) * LANES)
+            valued = qkv[page, :, 2 * width + pair * LANES : 2 * width + (pair + 1) * LANES]
+            got = dot_nn(square_low[pair % 2], valued)
+            context[page, :, cols] = jnp.where(side, got[:rows], got[rows:]).astype(low)
+
+        scores_of(0)
+        for pair in range(pairs):
+            if pair + 1 < pairs:
+                scores_of(pair + 1)
+            for at in range(0, 2 * rows, block):
+                scores = jnp.where(live, square[pair % 2, at : at + block], masked_score)
+                raised = jnp.exp(scores - jnp.max(scores, axis=-1, keepdims=True))
+                share = raised * (1.0 / jnp.sum(raised, axis=-1, keepdims=True))
+                chance[page, 2 * pair + at // rows, at % rows : at % rows + block] = share
+                square_low[pair % 2, at : at + block] = share.astype(low)
+            if pair > 0:
+                attend(pair - 1)
+        attend(pairs - 1)
 
         @pl.when(page == 0)
         def _():
@@ -269,30 +282,32 @@
             loads[2].wait()
             loads[3].wait()
 
-        for at in range(0, ff, chunk):
-            cols = slice(at, at + chunk)
-            before = dot_nn(normed_low[page], w_up[:, cols]) + bias[:, cols]
-            below, density = normal_terms(before)
-            hidden[page, :, cols] = (before * below).astype(low)
-            slope[page, :, cols] = (below + density).astype(slope.dtype)
+        for part in range(2):
+            mine = slice(part * tall, (part + 1) * tall)
+            for at in range(0, ff, chunk):
+                cols = slice(at, at + chunk)
+                before = dot_nn(normed_low[page, mine], w_up[:, cols]) + bias[:, cols]
+                below, density = normal_terms(before)
+                hidden[page, mine, cols] = (before * below).astype(low)
+                slope[page, mine, cols] = (below + density).astype(slope.dtype)
+            work[mine] = dot_nn(hidden[page, mine], w_down[...])
+            for at in range(part * tall, (part + 1) * tall, block):
+                here = slice(at, at + block)
+                normal, scale = norm_rows(normed[here] + (work[here] + offsets[4]))
+                normal_two[page, here] = normal
+                scale_two[page, here] = scale
+                result[pl.ds(pl.multiple_of(page * rows + at, block), block), :] = (
+                    normal * gains[1:2] + offsets[5]).astype(low)
+
+            @pl.when(first)
+            def _():
+                result_copy(page, part).start()
+
         if exchange:
             @pl.when(first)
             def _():
                 for copy in near_copies(page)[:-1]:
                     copy.start()
-
-        work[...] = dot_nn(hidden[page], w_down[...])
-        for at in range(0, rows, block):
-            here = slice(at, at + block)
-            normal, scale = norm_rows(normed[here] + (work[here] + offsets[4]))
-            normal_two[page, here] = normal
-            scale_two[page, here] = scale
-            result[pl.ds(pl.multiple_of(page * rows + at, block), block), :] = (
-                normal * gains[1:2] + offsets[5]).astype(low)
-
-        @pl.when(first)
-        def _():
-            result_copy(page).start()
 
         return carry
 
@@ -382,36 +397,47 @@
         def _():
             right_copies(page - 1)[4].wait()
 
-        for pair in range(pairs):
+        def upstream_of(pair):
+            valued = qkv[page, :, 2 * width + pair * LANES : 2 * width + (pair + 1) * LANES]
+            given = d_context[:, pair * LANES : (pair + 1) * LANES]
+            parts = [jnp.where(side, given, zero), jnp.where(side, zero, given)]
+            square[pair % 2] = dot_nt(jnp.concatenate(parts, axis=0), valued)
+
+        def consume(pair):
             cols = slice(pair * LANES, (pair + 1) * LANES)
             keyed = jnp.concatenate([qkv[page, :, width + pair * LANES : width + (pair + 1) * LANES], mark], axis=1)
-            valued = qkv[page, :, 2 * width + pair * LANES : 2 * width + (pair + 1) * LANES]
-            given = d_context[:, cols]
-            for half in range(2):
-                mine = jnp.where(side if half == 0 else ~side, given, zero)
-                square[half] = dot_nt(mine, valued)
             found = []
+            joined = dot_nn(square_low[pair % 2], keyed)
             for half in range(2):
                 head = 2 * pair + half
-                for at in range(0, rows, block):
-                    share = chance[page, head, at : at + block]
-                    both = share * square[half, at : at + block]
-                    d_scores = both - share * jnp.sum(both, axis=-1, keepdims=True)
-                    square_low[half, at : at + block] = d_scores.astype(low)
-            for half in range(2):
-                head = 2 * pair + half
-                slim = slice(head * size, (head + 1) * size)
-                both = dot_nn(square_low[half], keyed)
+                slim_rows = slice(head * size, (head + 1) * size)
+                both = joined[half * rows : (half + 1) * rows]
                 found.append(both[:, :LANES])
                 rest = both[:, LANES:]
                 upper = rest.astype(low)
                 lower = (rest - upper.astype(high)).astype(low)
                 cross[:, 2 * head * LANES : (2 * head + 1) * LANES] = upper
                 cross[:, (2 * head + 1) * LANES : (2 * head + 2) * LANES] = lower
-                back[slim, :] = dot_nn(turned[slim, :], square_low[half]) * scaling
+                back[slim_rows, :] = dot_nn(turned[slim_rows, :], square_low[pair % 2, half * rows : (half + 1) * rows]) * scaling
                 back[slice(width + head * size, width + (head + 1) * size), :] = dot_nn(
-                    turned_grad[slim, :], chance[page, head].astype(low))
+                    turned_grad[slim_rows, :], chance[page, head].astype(low))
             d_proj[:, cols] = (jnp.where(side, found[0], found[1]) * scaling).astype(low)
+
+        upstream_of(0)
+        for pair in range(pairs):
+            if pair + 1 < pairs:
+                upstream_of(pair + 1)
+            for half in range(2):
+                head = 2 * pair + half
+                for at in range(0, rows, block):
+                    here = slice(half * rows + at, half * rows + at + block)
+                    share = chance[page, head, at : at + block]
+                    both = share * square[pair % 2, here]
+                    d_scores = both - share * jnp.sum(both, axis=-1, keepdims=True)
+                    square_low[pair % 2, here] = d_scores.astype(low)
+            if pair > 0:
+                consume(pair - 1)
+        consume(pairs - 1)
         d_proj[:, width:] = back[...].astype(low).T
         sums[2] += column_sum(d_proj[:, 0:width])
         sums[3] += column_sum(d_proj[:, 2 * width :])
@@ -453,7 +479,8 @@
     for page in range(pages):
         @pl.when(first)
         def _():
-            result_copy(page).wait_send()
+            for part in range(2):
+                result_copy(page, part).wait_send()
 
         @pl.when(section == 1)
         def _():
@@ -481,7 +508,7 @@
         VM((pages, rows, width), high), VM((pages, rows, 1), high),
         VM((rows, heads * LANES), low),
         VM((rows, width), high),
-        VM((2, rows, rows), high), VM((2, rows, rows), low),
+        VM((2, 2 * rows, rows), high), VM((2, 2 * rows, rows), low),
         VM((rows, 2 * heads * LANES), low),
         VM((rows, 3 * width), low), VM((rows, width), low), VM((rows, ff), low), VM((pages, rows, width), low),
         VM((width, rows), low), VM((width, rows), low), VM((2 * width, rows), high),
@@ -489,7 +516,7 @@
         VM((pages * rows, LANES), low), VM((heads, LANES, LANES), low),
         VM((pages, rows, ff // 2), low), VM((2, width, pages * rows), low),
         pltpu.SemaphoreType.DMA((4,)), pltpu.SemaphoreType.DMA((pages,)), pltpu.SemaphoreType.DMA((2, 2 * ff // width)),
-        pltpu.SemaphoreType.DMA((pages + 5,)), pltpu.SemaphoreType.DMA((2 * pages,)), pltpu.SemaphoreType.DMA((2 * pages,)),
+        pltpu.SemaphoreType.DMA((pages + 5,)), pltpu.SemaphoreType.DMA((3 * pages,)), pltpu.SemaphoreType.DMA((3 * pages,)),
         pltpu.SemaphoreType.DMA((pages, ff // width + 1)), pltpu.SemaphoreType.DMA((pages, ff // width + 1)),
     ]
     return pl.pallas_call(

time: 168 us -> 162 us (0.964)
  Pallas kernels: 167 us -> 161 us
    pallas_call x1, Pallas kernels: 82.6 us -> 76.7 us  [both_passes(): pl.pallas_call(functools.partial(main_kernel, sizes, exchange), out_shape...]
where the time goes in v3:
time: 162 us; the launch traced here: 161 us
  Pallas kernels  161 us (99%)
    pallas_call x1, Pallas kernels, reduce_grads(): pl.pallas_call(functools.partial(rs_kernel, count, levels, rows, cols, la...  80.4 us
    pallas_call x1, Pallas kernels, both_passes(): pl.pallas_call(functools.partial(main_kernel, sizes, exchange), out_shape...  76.7 us
    pallas_call x1, Pallas kernels, settle(): pl.pallas_call(functools.partial(settle_kernel, len(arrays)), out_shape=t...  3.57 us

profile of v3, /device:TPU:0, one launch (start us, length us, event | category | flops | bytes accessed | tf_op | source)
XLA Modules:
  0.0 161.5 jit_solution(11291223533774432374)
XLA Ops:
  0.6 76.7 %shard_map.195 = (bf16[512,768]{1,0:T(8,128)(2,1)}, f32[512,768]{1,0:T(8,128)}, bf16[2304,512]{1,0:T(8,128)(2,1)}, bf16[4,384,1024]{2,1,0:T(8,128)(2,1)}, bf16[4...) custom-call(s32[2]{0:T(128)} %lengths.1, ...), custom_call_target="tpu_custom_call" | custom-call | tf_op jit(solution)/shard_map/pallas_call | solution.py:522
  77.3 80.4 %shard_map.196 = (f32[1,48,2304]{2,1,0:T(8,128)}, f32[1,48,768]{2,1,0:T(8,128)}, f32[1,48,3072]{2,1,0:T(8,128)}, f32[1,192,768]{2,1,0:T(8,128)}, f32[3,12,1,64]{...) custom-call(bf16[2304,512]{1,0:T(8,128)(2,1)} %get-tuple-element.40.plain_hbm, ...), custom_call_target="tpu_custom_call" | custom-call | tf_op jit(solution)/shard_map/pallas_call | solution.py:945
  157.7 3.6 %shard_map.197 = (bf16[1,512,768]{2,1,0:T(8,128)(2,1)}, f32[1,512,768]{2,1,0:T(8,128)}, f32[1,48,2304]{2,1,0:T(8,128)}, f32[1,48,768]{2,1,0:T(8,128)}, f32[1,48,...) custom-call(bf16[1,512,768]{2,1,0:T(8,128)(2,1)} %bitcast.16, ...), custom_call_target="tpu_custom_call" | custom-call | tf_op jit(solution)/shard_map/pallas_call | solution.py:973

commit v4 on v3

--- a/solution.py
+++ b/solution.py
@@ -200,8 +200,9 @@
         here = pl.ds(pl.multiple_of(page * rows + part * tall, tall), tall)
         return peer_copy(result.at[here], arrive.at[page, pl.ds(part * tall, tall)], 2 * page + part)
 
-    def grad_copy(page):
-        return peer_copy(sent_grad.at[page], arrive_grad.at[page], 2 * pages + page)
+    def grad_copy(page, part):
+        here = pl.ds(part * tall, tall)
+        return peer_copy(sent_grad.at[page, here], arrive_grad.at[page, here], 2 * pages + 2 * page + part)
 
     def forward(page, carry):
         @pl.when(first)
@@ -282,26 +283,34 @@
             loads[2].wait()
             loads[3].wait()
 
-        for part in range(2):
-            mine = slice(part * tall, (part + 1) * tall)
-            for at in range(0, ff, chunk):
-                cols = slice(at, at + chunk)
-                before = dot_nn(normed_low[page, mine], w_up[:, cols]) + bias[:, cols]
-                below, density = normal_terms(before)
-                hidden[page, mine, cols] = (before * below).astype(low)
-                slope[page, mine, cols] = (below + density).astype(slope.dtype)
-            work[mine] = dot_nn(hidden[page, mine], w_down[...])
-            for at in range(part * tall, (part + 1) * tall, block):
-                here = slice(at, at + block)
-                normal, scale = norm_rows(normed[here] + (work[here] + offsets[4]))
-                normal_two[page, here] = normal
-                scale_two[page, here] = scale
-                result[pl.ds(pl.multiple_of(page * rows + at, block), block), :] = (
-                    normal * gains[1:2] + offsets[5]).astype(low)
-
-            @pl.when(first)
-            def _():
-                result_copy(page, part).start()
+        def feed_forward(parts):
+            high_rows = rows // parts
+            for part in range(parts):
+                mine = slice(part * high_rows, (part + 1) * high_rows)
+                for at in range(0, ff, chunk):
+                    cols = slice(at, at + chunk)
+                    before = dot_nn(normed_low[page, mine], w_up[:, cols]) + bias[:, cols]
+                    below, density = normal_terms(before)
+                    hidden[page, mine, cols] = (before * below).astype(low)
+                    slope[page, mine, cols] = (below + density).astype(slope.dtype)
+                work[mine] = dot_nn(hidden[page, mine], w_down[...])
+                for at in range(part * high_rows, (part + 1) * high_rows, block):
+                    here = slice(at, at + block)
+                    normal, scale = norm_rows(normed[here] + (work[here] + offsets[4]))
+                    normal_two[page, here] = normal
+                    scale_two[page, here] = scale
+                    result[pl.ds(pl.multiple_of(page * rows + at, block), block), :] = (
+                        normal * gains[1:2] + offsets[5]).astype(low)
+                if parts == 2:
+                    result_copy(page, part).start()
+
+        @pl.when(first)
+        def _():
+            feed_forward(2)
+
+        @pl.when(section == 1)
+        def _():
+            feed_forward(1)
 
         if exchange:
             @pl.when(first)
@@ -328,7 +337,8 @@
     def backward(page, carry):
         @pl.when(first)
         def _():
-            grad_copy(page).wait_recv()
+            for part in range(2):
+                grad_copy(page, part).wait_recv()
 
         @pl.when(section == 1)
         def _():
@@ -445,18 +455,29 @@
             vectors[row : row + 1, :] += value
         right_copies(page)[0].start()
         right_copies(page)[4].start()
-        work[...] = dot_nt(d_proj[...], w_in[...])
-        for at in range(0, rows, block):
-            here = slice(at, at + block)
-            d_in = d_first[here] + work[here]
-            narrow = d_in.astype(low)
-            sent_grad[page, here] = narrow
-            input_grads[pl.ds(pl.multiple_of(page * rows + at, block), block), :] = jnp.where(
-                first, d_in, narrow.astype(high))
+        def input_grad(parts):
+            high_rows = rows // parts
+            for part in range(parts):
+                mine = slice(part * high_rows, (part + 1) * high_rows)
+                work[mine] = dot_nt(d_proj[mine], w_in[...])
+                for at in range(part * high_rows, (part + 1) * high_rows, block):
+                    here = slice(at, at + block)
+                    d_in = d_first[here] + work[here]
+                    narrow = d_in.astype(low)
+                    if parts == 2:
+                        sent_grad[page, here] = narrow
+                        d_in = narrow.astype(high)
+                    input_grads[pl.ds(pl.multiple_of(page * rows + at, block), block), :] = d_in
+                if parts == 2:
+                    grad_copy(page, part).start()
+
+        @pl.when(first)
+        def _():
+            input_grad(1)
 
         @pl.when(section == 1)
         def _():
-            grad_copy(page).start()
+            input_grad(2)
 
         return carry
 
@@ -484,7 +505,8 @@
 
         @pl.when(section == 1)
         def _():
-            grad_copy(page).wait_send()
+            for part in range(2):
+                grad_copy(page, part).wait_send()
 
 
 def both_passes(tokens, cotangent, lengths, buckets, layout, params, exchange):
@@ -516,7 +538,7 @@
         VM((pages * rows, LANES), low), VM((heads, LANES, LANES), low),
         VM((pages, rows, ff // 2), low), VM((2, width, pages * rows), low),
         pltpu.SemaphoreType.DMA((4,)), pltpu.SemaphoreType.DMA((pages,)), pltpu.SemaphoreType.DMA((2, 2 * ff // width)),
-        pltpu.SemaphoreType.DMA((pages + 5,)), pltpu.SemaphoreType.DMA((3 * pages,)), pltpu.SemaphoreType.DMA((3 * pages,)),
+        pltpu.SemaphoreType.DMA((pages + 5,)), pltpu.SemaphoreType.DMA((4 * pages,)), pltpu.SemaphoreType.DMA((4 * pages,)),
         pltpu.SemaphoreType.DMA((pages, ff // width + 1)), pltpu.SemaphoreType.DMA((pages, ff // width + 1)),
     ]
     return pl.pallas_call(
@@ -573,19 +595,19 @@
         jnp.where(place < 2 * BUCKETS, found[BUCKETS : 2 * BUCKETS], found[2 * BUCKETS : 3 * BUCKETS]))
 
 
-LAGS = ((0, 2, 7, 12, 17), (0, 1, 3, 8, 13))
+LAGS = ((0, 3, 9, 13, 18), (0, 1, 3, 6, 11))
 
 
 def down_turn(turn):
-    return jnp.logical_or(turn == 35, jnp.logical_and(turn < 33, turn % 3 == 0))
+    return jnp.where(turn < 12, turn % 2 == 0, turn % 4 == 0)
 
 
 def down_of(turn):
-    return jnp.where(turn == 35, 11, turn // 3)
+    return jnp.where(turn < 12, turn // 2, 3 + turn // 4)
 
 
 def place_of(turn):
-    other = jnp.where(turn < 33, 2 * (turn // 3) + turn % 3 - 1, turn - 11)
+    other = jnp.where(turn < 12, turn // 2, turn - 6 - (turn - 9) // 4)
     other = jnp.where(other < 12, other + 12, jnp.where(other < 15, other - 3, other - 15))
     return jnp.where(down_turn(turn), 24 + down_of(turn), other)
 
@@ -696,7 +718,7 @@
         return jnp.logical_and(first, down_turn(turn))
 
     def far_first(turn):
-        return jnp.logical_and(section == 1, turn % 6 == 0)
+        return jnp.logical_and(section == 1, turn % 6 == 2)
 
     def start(turn):
         at = place_of(turn)

time: 162 us -> 161 us (level)
  no operation moved by 1% of the time
where the time goes in v4:
time: 161 us
  Pallas kernels  160 us (99%)
    pallas_call x1, Pallas kernels, reduce_grads(): pl.pallas_call(functools.partial(rs_kernel, count, levels, rows, cols, la...  79.2 us
    pallas_call x1, Pallas kernels, both_passes(): pl.pallas_call(functools.partial(main_kernel, sizes, exchange), out_shape...  76.9 us
    pallas_call x1, Pallas kernels, settle(): pl.pallas_call(functools.partial(settle_kernel, len(arrays)), out_shape=t...  3.57 us

profile of v4, /device:TPU:0, one launch (start us, length us, event | category | flops | bytes accessed | tf_op | source)
XLA Modules:
  0.0 160.6 jit_solution(1986600642495798590)
XLA Ops:
  0.6 76.9 %shard_map.195 = (bf16[512,768]{1,0:T(8,128)(2,1)}, f32[512,768]{1,0:T(8,128)}, bf16[2304,512]{1,0:T(8,128)(2,1)}, bf16[4,384,1024]{2,1,0:T(8,128)(2,1)}, bf16[4...) custom-call(s32[2]{0:T(128)} %lengths.1, ...), custom_call_target="tpu_custom_call" | custom-call | tf_op jit(solution)/shard_map/pallas_call | solution.py:544
  77.6 79.2 %shard_map.196 = (f32[1,48,2304]{2,1,0:T(8,128)}, f32[1,48,768]{2,1,0:T(8,128)}, f32[1,48,3072]{2,1,0:T(8,128)}, f32[1,192,768]{2,1,0:T(8,128)}, f32[3,12,1,64]{...) custom-call(bf16[2304,512]{1,0:T(8,128)(2,1)} %get-tuple-element.40.plain_hbm, ...), custom_call_target="tpu_custom_call" | custom-call | tf_op jit(solution)/shard_map/pallas_call | solution.py:967
  156.8 3.6 %shard_map.197 = (bf16[1,512,768]{2,1,0:T(8,128)(2,1)}, f32[1,512,768]{2,1,0:T(8,128)}, f32[1,48,2304]{2,1,0:T(8,128)}, f32[1,48,768]{2,1,0:T(8,128)}, f32[1,48,...) custom-call(bf16[1,512,768]{2,1,0:T(8,128)(2,1)} %bitcast.16, ...), custom_call_target="tpu_custom_call" | custom-call | tf_op jit(solution)/shard_map/pallas_call | solution.py:995

commit v5 on v4

--- a/solution.py
+++ b/solution.py
@@ -51,12 +51,12 @@
     sizes, exchange,
     lengths, tokens, cotangent, buckets, layout, gains, offsets, bias,
     in_hbm, out_hbm, up_hbm, down_hbm,
-    result, input_grads, plain_hbm, pair_hbm, full_hbm, right_hbm, cross_hbm, vectors, bias_grad, near_branch,
+    result_hbm, input_grads_hbm, plain_hbm, pair_hbm, full_hbm, right_hbm, cross_hbm, vectors, bias_grad, near_branch,
     w_in, w_out, w_up, w_down, arrive, arrive_grad, sent_grad,
     qkv, chance, context, normal_one, scale_one, normed, normed_low, slope, hidden,
     normal_two, scale_two, picked, work, square, square_low, cross, d_proj, d_att, d_before, d_branch,
-    turned, turned_grad, back, d_context, d_first, onehot, spread, near_hidden, spun,
-    load_sem, page_sem, spun_sem, right_sem, send_sem, recv_sem, near_send, near_recv,
+    turned, turned_grad, back, d_context, d_first, onehot, spread, near_hidden, spun, result, input_grads,
+    load_sem, page_sem, spun_sem, right_sem, send_sem, recv_sem, near_send, near_recv, final_sem,
 ):
     rows, width, heads, ff, pages = sizes
     size = width // heads
@@ -195,6 +195,12 @@
     side = lane < size
 
     tall = rows // 2
+
+    def final_copies(page):
+        return [
+            pltpu.make_async_copy(source.at[page_rows(page)], target.at[page_rows(page)], final_sem.at[slot, page])
+            for slot, (source, target) in enumerate(((result, result_hbm), (input_grads, input_grads_hbm)))
+        ]
 
     def result_copy(page, part):
         here = pl.ds(pl.multiple_of(page * rows + part * tall, tall), tall)
@@ -312,6 +318,7 @@
         def _():
             feed_forward(1)
 
+        final_copies(page)[0].start()
         if exchange:
             @pl.when(first)
             def _():
@@ -335,46 +342,57 @@
             turn_slabs(2 * ff // width, False, 0)
 
     def backward(page, carry):
+        @pl.when(section == 1)
+        def _():
+            own_grad_copy(page).wait()
+
+        sums = [jnp.zeros((1, width), high) for _ in range(8)]
+
+        @pl.when(page > 0)
+        def _():
+            right_copies(page - 1)[2].wait()
+
+        def feed_back(parts):
+            high_rows = rows // parts
+            totals = {1: 0.0, 6: 0.0, 7: 0.0}
+            for part in range(parts):
+                if parts == 2:
+                    grad_copy(page, part).wait_recv()
+                mine = slice(part * high_rows, (part + 1) * high_rows)
+                for at in range(part * high_rows, (part + 1) * high_rows, block):
+                    here = slice(at, at + block)
+                    upstream = arrive_grad[page, here].astype(high)
+                    normal = normal_two[page, here]
+                    totals[1] += column_sum(upstream * normal)
+                    totals[7] += column_sum(upstream)
+                    d_second = norm_back(upstream, gains[1:2], normal, scale_two[page, here])
+                    d_first[here] = d_second
+                    branch = d_second.astype(low)
+                    totals[6] += column_sum(branch)
+                    d_branch[page, here] = branch
+                if part == parts - 1:
+                    right_copies(page)[3].start()
+                    if exchange and parts == 2:
+                        near_copies(page)[-1].start()
+                for at in range(0, ff, chunk):
+                    cols = slice(at, at + chunk)
+                    d_hidden = dot_nt(d_branch[page, mine], w_down[cols, :])
+                    d_chunk = (d_hidden * slope[page, mine, cols].astype(high)).astype(low)
+                    d_before[mine, cols] = d_chunk
+                    bias_grad[:, cols] += column_sum(d_chunk)
+                work[mine] = dot_nt(d_before[mine], w_up[...])
+            for row, value in totals.items():
+                vectors[row : row + 1, :] += value
+
         @pl.when(first)
         def _():
-            for part in range(2):
-                grad_copy(page, part).wait_recv()
+            feed_back(2)
 
         @pl.when(section == 1)
         def _():
-            own_grad_copy(page).wait()
-
-        sums = [jnp.zeros((1, width), high) for _ in range(8)]
-        for at in range(0, rows, block):
-            here = slice(at, at + block)
-            upstream = arrive_grad[page, here].astype(high)
-            normal = normal_two[page, here]
-            sums[1] += column_sum(upstream * normal)
-            sums[7] += column_sum(upstream)
-            d_second = norm_back(upstream, gains[1:2], normal, scale_two[page, here])
-            d_first[here] = d_second
-            branch = d_second.astype(low)
-            sums[6] += column_sum(branch)
-            d_branch[page, here] = branch
-        right_copies(page)[3].start()
-        if exchange:
-            @pl.when(first)
-            def _():
-                near_copies(page)[-1].start()
-
-
-        @pl.when(page > 0)
-        def _():
-            right_copies(page - 1)[2].wait()
-
-        for at in range(0, ff, chunk):
-            cols = slice(at, at + chunk)
-            d_hidden = dot_nt(d_branch[page], w_down[cols, :])
-            d_chunk = (d_hidden * slope[page, :, cols].astype(high)).astype(low)
-            d_before[:, cols] = d_chunk
-            bias_grad[:, cols] += column_sum(d_chunk)
+            feed_back(1)
+
         right_copies(page)[2].start()
-        work[...] = dot_nt(d_before[...], w_up[...])
 
         @pl.when(page > 0)
         def _():
@@ -479,6 +497,7 @@
         def _():
             input_grad(2)
 
+        final_copies(page)[1].start()
         return carry
 
     lax.fori_loop(0, pages, backward, 0)
@@ -490,6 +509,8 @@
 
     for page in range(pages):
         right_copies(page)[3].wait()
+        for copy in final_copies(page):
+            copy.wait()
         if exchange:
             @pl.when(first)
             def _():
@@ -537,9 +558,11 @@
         VM((rows, width), low), VM((rows, width), high),
         VM((pages * rows, LANES), low), VM((heads, LANES, LANES), low),
         VM((pages, rows, ff // 2), low), VM((2, width, pages * rows), low),
+        VM(tokens.shape, low), VM(tokens.shape, high),
         pltpu.SemaphoreType.DMA((4,)), pltpu.SemaphoreType.DMA((pages,)), pltpu.SemaphoreType.DMA((2, 2 * ff // width)),
         pltpu.SemaphoreType.DMA((pages + 5,)), pltpu.SemaphoreType.DMA((4 * pages,)), pltpu.SemaphoreType.DMA((4 * pages,)),
         pltpu.SemaphoreType.DMA((pages, ff // width + 1)), pltpu.SemaphoreType.DMA((pages, ff // width + 1)),
+        pltpu.SemaphoreType.DMA((2, pages)),
     ]
     return pl.pallas_call(
         functools.partial(main_kernel, sizes, exchange),
@@ -556,7 +579,7 @@
             jax.ShapeDtypeStruct((pages * rows, width), low),
         ),
         in_specs=[pl.BlockSpec(memory_space=pltpu.SMEM), there, there, here, here, here, here, here] + [there] * 4,
-        out_specs=(here, here, there, there, there, there, there, here, here, there),
+        out_specs=(there,) * 7 + (here, here, there),
         scratch_shapes=scratch,
         compiler_params=pltpu.CompilerParams(
             collective_id=0, has_side_effects=True, vmem_limit_bytes=63 * 2**20),

time: 161 us -> 160 us (level)
  no operation moved by 1% of the time
where the time goes in v5:
time: 160 us
  Pallas kernels  159 us (99%)
    pallas_call x1, Pallas kernels, reduce_grads(): pl.pallas_call(functools.partial(rs_kernel, count, levels, rows, cols, la...  79.2 us
    pallas_call x1, Pallas kernels, both_passes(): pl.pallas_call(functools.partial(main_kernel, sizes, exchange), out_shape...  76.1 us
    pallas_call x1, Pallas kernels, settle(): pl.pallas_call(functools.partial(settle_kernel, len(arrays)), out_shape=t...  3.57 us

profile of v5, /device:TPU:0, one launch (start us, length us, event | category | flops | bytes accessed | tf_op | source)
XLA Modules:
  0.0 159.8 jit_solution(2864560614601825402)
XLA Ops:
  0.6 76.1 %shard_map.195 = (bf16[512,768]{1,0:T(8,128)(2,1)}, f32[512,768]{1,0:T(8,128)}, bf16[2304,512]{1,0:T(8,128)(2,1)}, bf16[4,384,1024]{2,1,0:T(8,128)(2,1)}, bf16[4...) custom-call(s32[2]{0:T(128)} %lengths.1, ...), custom_call_target="tpu_custom_call" | custom-call | tf_op jit(solution)/shard_map/pallas_call | solution.py:567
  76.8 79.2 %shard_map.196 = (f32[1,48,2304]{2,1,0:T(8,128)}, f32[1,48,768]{2,1,0:T(8,128)}, f32[1,48,3072]{2,1,0:T(8,128)}, f32[1,192,768]{2,1,0:T(8,128)}, f32[3,12,1,64]{...) custom-call(bf16[2304,512]{1,0:T(8,128)(2,1)} %get-tuple-element.40.plain_hbm, ...), custom_call_target="tpu_custom_call" | custom-call | tf_op jit(solution)/shard_map/pallas_call | solution.py:990
  156.0 3.6 %shard_map.197 = (bf16[1,512,768]{2,1,0:T(8,128)(2,1)}, f32[1,512,768]{2,1,0:T(8,128)}, f32[1,48,2304]{2,1,0:T(8,128)}, f32[1,48,768]{2,1,0:T(8,128)}, f32[1,48,...) custom-call(bf16[1,512,768]{2,1,0:T(8,128)(2,1)} %bitcast.16, ...), custom_call_target="tpu_custom_call" | custom-call | tf_op jit(solution)/shard_map/pallas_call | solution.py:1018
